TPU v7x, 256 devices: a whole 4x4x8 slice. The times are simulated.
256 devices in a mesh: view: 4 (over y), frame: 16 (over x_hi, z), band: 4 (over x_lo, core).
Axes of the slice: x: 4 (x_hi: 2, x_lo: 2; x = x_hi * 2 + x_lo), y: 4, z: 8, core: 2. Of those that a mesh axis runs over, the one named last changes fastest.
Arguments:
- hidden: bfloat16 [4, 16, 32, 64, 1152], P('view', 'frame', 'band'), may hold values from -6 to 6
- cond_queries: bfloat16 [4, 16, 32, 64, 1152], P('view', 'frame', 'band')
- cond_kv: bfloat16 [4, 16, 32, 64, 2304], P('view', 'frame', 'band'), may hold values from -6 to 6
- layout_kv: bfloat16 [16, 512, 2304], P('frame', 'band')
- layout_count: int32 [16, 4], P('frame'), may hold values from 1 to 128, 320 in all within a row
- intersection: int32 [4, 2], P('view'), may hold values from 16 to 32
- norm_gain: float32 [1152], replicated, may hold values from 0.1 to 1.9
- w_qkv: bfloat16 [1152, 3456], replicated
Outputs:
- temporal_heads: bfloat16 [4, 16, 32, 64, 1152], P('view', 'frame', 'band')
Inputs may be any that keep to these rules, and one draw needn't show every extreme that they name: `layout_count`: for each frame the counts sum to 320 and the largest is 128.
All inputs are finite; a program needn't handle non-finite values.
Results may differ from a plain program's by a relative error of at most 0.015.
Values may be sent and summed in bfloat16 or wider, within the bound.
No kernel may reach another device: no remote copies, remote signals or barrier semaphores. Data moves between devices by JAX's collectives and lax.ppermute only.
A program may use at most 192 MiB of HBM per device.

v0:
```python
import math

import jax
import jax.numpy as jnp
from jax import lax
from jax.sharding import PartitionSpec as P

HEADS = 16


epsilon = 1e-06


def passed_along(array, axis, by):
    length = lax.axis_size(axis)
    return lax.ppermute(array, axis, [(i, (i + by) % length) for i in range(length)])


def softmax_rows(scores):
    row_max = jnp.max(scores, axis=-1, keepdims=True)
    exponent = jnp.exp(scores - row_max)
    return (exponent / jnp.sum(exponent, axis=-1, keepdims=True)).astype(jnp.bfloat16)


def attend(queries, keys_values, key_live):
    model_width = queries.shape[-1]
    head_dim = model_width // HEADS
    key_count = keys_values.shape[0]
    query_heads = queries.reshape(-1, HEADS, head_dim)
    key_heads = keys_values[:, :model_width].reshape(key_count, HEADS, head_dim)
    value_heads = keys_values[:, model_width:].reshape(key_count, HEADS, head_dim)
    scores = jnp.einsum("qhe,khe->hqk", query_heads, key_heads, preferred_element_type=jnp.float32)
    scores = scores * (1.0 / math.sqrt(head_dim))
    scores = jnp.where(key_live[None, None, :], scores, -1e30)
    weights = softmax_rows(scores)
    mixed_rows = jnp.einsum(
        "hqk,khe->qhe", weights, value_heads, preferred_element_type=jnp.float32
    )
    return mixed_rows.reshape(-1, model_width)


def temporal(packed):
    frame_count, positions = (packed.shape[0], packed.shape[1])
    model_width = packed.shape[2] // 3
    head_dim = model_width // HEADS
    query_heads = packed[:, :, :model_width].reshape(frame_count, positions, HEADS, head_dim)
    key_heads = packed[:, :, model_width : 2 * model_width].reshape(
        frame_count, positions, HEADS, head_dim
    )
    value_heads = packed[:, :, 2 * model_width :].reshape(frame_count, positions, HEADS, head_dim)
    scores = jnp.einsum(
        "fphe,gphe->phfg", query_heads, key_heads, preferred_element_type=jnp.float32
    )
    weights = softmax_rows(scores * (1.0 / math.sqrt(head_dim)))
    result = jnp.einsum("phfg,gphe->fphe", weights, value_heads, preferred_element_type=jnp.float32)
    return result.reshape(frame_count, positions, model_width).astype(jnp.bfloat16)


def temporal_items(grouped):
    return temporal(grouped[:, 0])[:, None]


def project(state_rows, norm_gain, w_qkv):
    values_f = state_rows.astype(jnp.float32)
    inverse = lax.rsqrt(jnp.mean(values_f * values_f, axis=-1, keepdims=True) + epsilon)
    normed = (values_f * inverse * norm_gain).astype(jnp.bfloat16)
    return jnp.dot(normed, w_qkv, preferred_element_type=jnp.float32).astype(jnp.bfloat16)


def per_device(
    hidden, cond_queries, cond_kv, layout_kv, layout_count, intersection, norm_gain, w_qkv
):
    patch_rows, patch_cols, model_width = (hidden.shape[2], hidden.shape[3], hidden.shape[4])
    half_cols = patch_cols // 2
    tokens = patch_rows * patch_cols
    frame_count = lax.axis_size("frame")
    per_frame = tokens // frame_count
    own_kv = cond_kv[0, 0]
    from_left = passed_along(own_kv[:, half_cols:, :], "view", 1)
    from_right = passed_along(own_kv[:, :half_cols, :], "view", -1)
    layout_all = lax.all_gather(layout_kv[0], "band", axis=0, tiled=True)
    layout_rows = layout_kv.shape[1]
    band_count = lax.axis_size("band")
    slot_index = jnp.arange(layout_rows * band_count, dtype=jnp.int32)
    slot_owner = (slot_index // layout_rows)[:, None] == jnp.arange(band_count, dtype=jnp.int32)[
        None, :
    ]
    slot_limit = jnp.sum(jnp.where(slot_owner, layout_count[0][None, :], 0), axis=1)
    layout_live = slot_index % layout_rows < slot_limit
    column = jnp.arange(half_cols, dtype=jnp.int32)
    left_live = jnp.tile(column + half_cols >= patch_cols - intersection[0, 0], patch_rows)
    right_live = jnp.tile(column < intersection[0, 1], patch_rows)
    keys_values = jnp.concatenate(
        [
            from_left.reshape(patch_rows * half_cols, 2 * model_width),
            from_right.reshape(patch_rows * half_cols, 2 * model_width),
            layout_all,
        ],
        axis=0,
    )
    key_live = jnp.concatenate([left_live, right_live, layout_live])
    mixed_rows = attend(cond_queries[0, 0].reshape(tokens, model_width), keys_values, key_live)
    state_rows = (
        hidden[0, 0].reshape(tokens, model_width).astype(jnp.float32) + mixed_rows
    ).astype(jnp.bfloat16)
    packed = project(state_rows, norm_gain, w_qkv)
    outgoing = packed.reshape(1, frame_count, per_frame, 3 * model_width)
    regrouped = temporal_items(
        lax.all_to_all(outgoing, "frame", split_axis=1, concat_axis=0, tiled=True)
    )
    returned = lax.all_to_all(regrouped, "frame", split_axis=0, concat_axis=1, tiled=True)
    return returned.reshape(1, 1, patch_rows, patch_cols, model_width)


def solution(mesh):
    in_specs = (
        P("view", "frame", "band", None, None),
        P("view", "frame", "band", None, None),
        P("view", "frame", "band", None, None),
        P("frame", "band", None),
        P("frame", None),
        P("view", None),
        P(),
        P(),
    )
    out_specs = P("view", "frame", "band", None, None)
    return jax.shard_map(
        per_device, mesh=mesh, in_specs=in_specs, out_specs=out_specs, check_vma=False
    )
```

profile of v0, /device:TPU:8, one launch (start us, length us, event | category | flops | bytes accessed | tf_op | source)
XLA Modules:
  0.0 300.7 jit_solution(6447649272749163491)
XLA Ops:
  7.3 3.3 %fusion.39 = (bf16[8,32,2304]{2,1,0:T(8,128)(2,1)}, bf16[8,32,2304]{2,1,0:T(8,128)(2,1)}) fusion(bf16[8,64,2304]{2,1,0:T(8,128)(2,1)} %bitcast.55), kind=kLoop, calls=%fused_computation.58 | loop fusion | bytes 4718592 | tf_op jit(solution)/shard_map/slice | solution.py:79
  12.8 4.8 %reshape.104 = f32[512,16,72]{2,1,0:T(8,128)} reshape(bf16[1,1,8,64,1152]{4,3,2,1,0:T(8,128)(2,1)S(1)} %copy-done.1) | data formatting | bytes 3538944 | tf_op jit(solution)/shard_map/convert_element_type | solution.py:104
  17.7 5.8 %reshape_reshape_squeeze.3 = bf16[512,16,72]{2,1,0:T(8,128)(2,1)} reshape(bf16[1,1,8,64,1152]{4,3,2,1,0:T(8,128)(2,1)} %param.9) | data formatting | bytes 2359296 | tf_op jit(solution)/shard_map/reshape;reshape;squeeze | solution.py:29
  25.5 4.9 %copy.45 = f32[512,16,72]{0,2,1:T(8,128)} copy(f32[512,16,72]{2,1,0:T(8,128)} %reshape.104) | data formatting | bytes 4718592 | tf_op jit(solution)/shard_map/convert_element_type | solution.py:104
  32.6 6.0 %collective-permute-done = bf16[8,32,2304]{2,1,0:T(8,128)(2,1)} collective-permute-done((bf16[8,32,2304]{2,1,0:T(8,128)(2,1)}, bf16[8,32,2304]{2,1,0:T(8,128)(2,1)}, u32[]{:S(2)}, u32[]{:S(2)}) %collective-permute-start) | collective-permute-done | bytes 1179680 | tf_op jit(solution)/shard_map/ppermute | solution.py:16
  39.9 5.8 %all-gather.3.cloned.1.call-done = bf16[1,512,2304]{2,1,0:T(8,128)(2,1)} async-done(((bf16[1,128,2304]{2,1,0:T(8,128)(2,1)}), bf16[1,512,2304]{2,1,0:T(8,128)(2,1)}) %all-gather.3.cloned.1.call-update) | async-done | bytes 2359312 | tf_op jit(solution)/shard_map/all_gather | solution.py:81
  45.7 2.5 pad_maximum_fusion
  48.2 2.5 fusion.37
  50.7 2.8 copy.41
  53.6 4.3 %copy.40 = bf16[1024,1152]{0,1:T(8,128)(2,1)} copy(bf16[1024,1152]{1,0:T(8,128)(2,1)} %get-tuple-element.6) | data formatting | bytes 4718592 | tf_op jit(solution)/shard_map/slice | solution.py:31
  57.9 14.7 %fusion.20 = f32[16,1024,512]{2,1,0:T(8,128)} fusion(bf16[1024,16,72]{0,2,1:T(8,128)(2,1)S(1)} %bitcast.49, bf16[512,16,72]{2,1,0:T(8,128)(2,1)} %reshape_reshape_squeeze.3), kind=kOutput, calls=%fused_computation.29 | convolution fusion | flops 1207959552 | bytes 37093376 | tf_op jit(solution)/shard_map/qhe,khe->hqk/dot_general | solution.py:32
  72.6 35.2 %fusion.41 = (f32[16,512]{1,0:T(8,128)S(1)}, f32[16,512,1024]{1,2,0:T(8,128)}) fusion(f32[16,1024,512]{2,1,0:T(8,128)} %fusion.20, pred[1024]{0:T(1024)(128)(4,1)S(1)} %pad_add_fusion), kind=kOutput, calls=%fused_computation.60 | output fusion | flops 50332672 | bytes 67142656 | tf_op jit(solution)/shard_map/sub | solution.py:21
  107.8 14.9 %multiply_reduce_fusion.1 = (f32[512]{0:T(512)S(1)}, f32[16,72,512]{2,1,0:T(8,128)}) fusion(f32[512,16,72]{0,2,1:T(8,128)S(1)} %copy-done.2, bf16[1024,16,72]{0,2,1:T(8,128)(2,1)} %bitcast.56, f32[16,512,1024]{1,2,0:T(8,128)} %get-tuple-element.15, f32[16,512]{1,0:T(8,128)S(1)} %get-tuple-element.14), kind=kOutput, calls=%fused_computation.23 | convolution fusion | flops 1227685376 | bytes 40667136 | tf_op jit(solution)/shard_map/hqk,khe->qhe/dot_general | solution.py:36
  122.7 2.1 fusion.13
  124.8 8.8 %convolution_convert_fusion = bf16[512,3456]{1,0:T(8,128)(2,1)S(1)} fusion(bf16[1152,3456]{1,0:T(8,128)(2,1)} %param.15, bf16[512,1152]{0,1:T(8,128)(2,1)S(1)} %fusion.13, f32[1152]{0:T(1024)S(1)} %copy-done.5, f32[512]{0:T(512)S(1)} %add_rsqrt_fusion), kind=kOutput, calls=%fused_computation.12 | convolution fusion | flops 4080992256 | bytes 12687872 | tf_op jit(solution)/shard_map/dot_general | solution.py:67
  133.6 91.4 %all_to_all.8 = bf16[1,16,32,3456]{3,2,0,1:T(8,128)(2,1)S(1)} all-to-all(bf16[1,16,32,3456]{3,2,0,1:T(8,128)(2,1)S(1)} %bitcast.54), channel_id=1, replica_groups=mesh['view'=4,'frame'=16,'band'=4] {'frame'}, dimensions={1} | all-to-all | bytes 7077888 | tf_op jit(solution)/shard_map/all_to_all | solution.py:109
  226.8 5.0 %reshape.100 = bf16[16,32,16,72]{3,2,1,0:T(8,128)(2,1)S(1)} reshape(bf16[16,32,1152]{2,1,0:T(8,128)(2,1)} %get-tuple-element.9) | data formatting | bytes 2359296 | tf_op jit(solution)/shard_map/reshape | solution.py:46
  231.8 5.7 %reshape.101 = bf16[16,32,16,72]{3,2,1,0:T(8,128)(2,1)} reshape(bf16[16,32,1152]{2,1,0:T(8,128)(2,1)} %get-tuple-element.8) | data formatting | bytes 2359296 | tf_op jit(solution)/shard_map/reshape | solution.py:47
  237.5 4.1 %fusion.17 = f32[32,16,16,16]{2,3,1,0:T(8,128)S(1)} fusion(bf16[16,32,16,72]{3,2,1,0:T(8,128)(2,1)} %reshape.101, bf16[16,32,16,72]{3,2,1,0:T(8,128)(2,1)S(1)} %reshape.100), kind=kOutput, calls=%fused_computation.26 | convolution fusion | flops 18874368 | bytes 2883584 | tf_op jit(solution)/shard_map/fphe,gphe->phfg/dot_general | solution.py:51
  241.6 3.5 %fusion.42 = (f32[32,16,16]{2,1,0:T(8,128)S(1)}, f32[32,16,16,16]{2,3,1,0:T(8,128)}) fusion(f32[32,16,16,16]{2,3,1,0:T(8,128)S(1)} %fusion.17), kind=kOutput, calls=%fused_computation.61 | output fusion | flops 524303 | bytes 1081344 | tf_op jit(solution)/shard_map/sub | solution.py:21
  245.1 3.7 %reshape.99 = bf16[16,32,16,72]{3,2,1,0:T(8,128)(2,1)S(1)} reshape(bf16[16,32,1152]{2,1,0:T(8,128)(2,1)S(1)} %get-tuple-element.7) | data formatting | bytes 2359296 | tf_op jit(solution)/shard_map/reshape | solution.py:50
  248.8 3.8 %convert_bitcast_fusion = bf16[16,32,16,72]{3,0,2,1:T(8,128)(2,1)S(1)} fusion(f32[32,16,16,16]{2,3,1,0:T(8,128)} %get-tuple-element.19, f32[32,16,16]{2,1,0:T(8,128)S(1)} %get-tuple-element.18, bf16[16,32,16,72]{3,2,1,0:T(8,128)(2,1)S(1)} %reshape.99), kind=kOutput, calls=%fused_computation.31 | convolution fusion | flops 19726336 | bytes 2916352 | tf_op jit(solution)/shard_map/phfg,gphe->fphe/dot_general | solution.py:55
  253.2 2.6 convert_element_type.66
  255.8 37.1 %all_to_all.9 = bf16[16,1,32,1152]{3,2,1,0:T(8,128)(2,1)S(1)} all-to-all(bf16[16,1,32,1152]{3,2,1,0:T(8,128)(2,1)S(1)} %bitcast.52), channel_id=1, replica_groups=mesh['view'=4,'frame'=16,'band'=4] {'frame'}, dimensions={0} | all-to-all | bytes 2359296 | tf_op jit(solution)/shard_map/all_to_all | solution.py:111
  (34 shorter events, 11.2 us)
Async XLA Ops:
  6.5 39.1 %all-gather.3.cloned.1.call-start = ((), (), s32[]{:S(2)}) async-start(), calls=%async_computation.2 | async-start | bytes 2949120 | tf_op jit(solution)/shard_map/all_gather | solution.py:81
  7.3 5.5 %copy-start.1 = (bf16[1,1,8,64,1152]{4,3,2,1,0:T(8,128)(2,1)S(1)}, bf16[1,1,8,64,1152]{4,3,2,1,0:T(8,128)(2,1)}, u32[]{:S(2)}) copy-start(bf16[1,1,8,64,1152]{4,3,2,1,0:T(8,128)(2,1)} %param.8) | copy-start | bytes 3538948
  10.6 28.0 %collective-permute-start = (bf16[8,32,2304]{2,1,0:T(8,128)(2,1)}, bf16[8,32,2304]{2,1,0:T(8,128)(2,1)}, u32[]{:S(2)}, u32[]{:S(2)}) collective-permute-start(bf16[8,32,2304]{2,1,0:T(8,128)(2,1)} %get-tuple-element.10), channel_id=1, source_target_pairs={{0,64},{64,128},{128,192},{192,0},{1,65},{65,129},{129,193},{193,1... | collective-permute-start | bytes 3538952 | tf_op jit(solution)/shard_map/ppermute | solution.py:16
  12.1 27.7 %collective-permute-start.1 = (bf16[8,32,2304]{2,1,0:T(8,128)(2,1)}, bf16[8,32,2304]{2,1,0:T(8,128)(2,1)}, u32[]{:S(2)}, u32[]{:S(2)}) collective-permute-start(bf16[8,32,2304]{2,1,0:T(8,128)(2,1)} %get-tuple-element.11), channel_id=1, source_target_pairs={{0,192},{64,0},{128,64},{192,128},{1,193},{65,1},{129,65},{193,129... | collective-permute-start | bytes 3538952 | tf_op jit(solution)/shard_map/ppermute | solution.py:16
  17.7 5.8 %copy-start.3 = (s32[1,2]{1,0:T(1,128)S(1)}, s32[1,2]{1,0:T(1,128)}, u32[]{:S(2)}) copy-start(s32[1,2]{1,0:T(1,128)} %param.13) | copy-start | bytes 28
  30.4 2.1 copy-start.4
  72.6 35.2 %copy-start.2 = (f32[512,16,72]{0,2,1:T(8,128)S(1)}, f32[512,16,72]{0,2,1:T(8,128)}, u32[]{:S(2)}) copy-start(f32[512,16,72]{0,2,1:T(8,128)} %copy.45) | copy-start | bytes 7077892
  107.8 14.9 %copy-start = (f32[512,1152]{0,1:T(8,128)S(1)}, f32[512,1152]{0,1:T(8,128)}, u32[]{:S(2)}) copy-start(f32[512,1152]{0,1:T(8,128)} %copy.44) | copy-start | bytes 7077892
  122.7 2.1 copy-start.5
Sparse Core Ops, SparseCore 0:
  9.2 36.4 all-gather.2
where the time goes:
time: 301 us
  blocking collectives  129 us (43%)
  local copies, waits for them, and re-layouts  51.5 us (17%)
  matrix products  46.3 us (15%)
  other arithmetic  44.2 us (15%)
  between operations  14.2 us (5%)
  waiting for transfers between devices  13.8 us (5%)
    all_to_all x1, blocking collectives, per_device(): lax.all_to_all(outgoing, 'frame', split_axis=1, concat_axis=0, tiled=True)  91.4 us
    sub x2, other arithmetic, softmax_rows(): exponent = jnp.exp(scores - row_max)  38.7 us
    all_to_all x1, blocking collectives, per_device(): lax.all_to_all(regrouped, 'frame', split_axis=0, concat_axis=1, tiled=True)  37.1 us
    dot_general x1, matrix products, attend(): jnp.einsum('hqk,khe->qhe', weights, value_heads, preferred_element_type=j...  14.9 us
    dot_general x1, matrix products, attend(): jnp.einsum('qhe,khe->hqk', query_heads, key_heads, preferred_element_type...  14.7 us
    convert_element_type x3, local copies, waits for them, and re-layouts, per_device(): hidden[0, 0].reshape(tokens, model_width).astype(jnp.float32) + mixed_rows  11.7 us
    dot_general x1, matrix products, project(): jnp.dot(normed, w_qkv, preferred_element_type=jnp.float32)  8.8 us
    ppermute x2, waiting for transfers between devices, passed_along(): lax.ppermute(array, axis, [(i, (i + by) % length) for i in range(length)])  7.28 us
  transfers between devices with their start and end apart: 3, of which 3 were waited for; matrix products, arithmetic and copies ran while one was open for 7% of the time, Pallas kernels for 0%

commit v1 on v0

v1 whole, which is shorter than its diff:
```python
import functools
import math

import jax
import jax.numpy as jnp
from jax import lax
from jax.experimental import pallas as pl
from jax.experimental.pallas import tpu as pltpu
from jax.sharding import PartitionSpec as P

HEADS = 16
LANES = 128
CHUNKS = 2
EPSILON = 1e-06
DEAD = -1e30
VMEM_LIMIT = 56 << 20
LOG2E = 1.4426950408889634
NT = (((1,), (1,)), ((), ()))


def head_span(head, width):
    size = width // HEADS
    low, high = head * size, (head + 1) * size
    return low, high, low // LANES * LANES, -(-high // LANES) * LANES


def head_mask(head, rows, width):
    low, high, first, last = head_span(head, width)
    column = lax.broadcasted_iota(jnp.int32, (rows, last - first), 1) + first
    return (column >= low) & (column < high)


def row_max(pieces):
    return functools.reduce(
        jnp.maximum, [jnp.max(piece, axis=1, keepdims=True) for piece in pieces]
    )


def lane_index(count):
    return lax.broadcasted_iota(jnp.int32, (1, count), 1)


def layout_kernel(band_ref, count_ref, q_ref, *refs):
    blocks = [(refs[2 * i], refs[2 * i + 1]) for i in range(4)]
    acc_ref, max_ref, sum_ref = refs[8:]
    rows, width = q_ref.shape
    scale = LOG2E / math.sqrt(width // HEADS)
    band = band_ref[0]
    slots = blocks[0][0].shape[0]
    biases = []
    for i in range(4):
        limit = count_ref[0, jnp.bitwise_xor(band, i)]
        biases.append(jnp.where(lane_index(slots) < limit, 0.0, DEAD))
    done = 0
    for head in range(HEADS):
        low, high, first, last = head_span(head, width)
        mask = head_mask(head, rows, width)
        query = jnp.where(mask, q_ref[:, first:last], jnp.bfloat16(0))
        scores = []
        for (key, _), bias in zip(blocks, biases):
            product = lax.dot_general(
                query, key[:, first:last], NT, preferred_element_type=jnp.float32
            )
            scores.append(product * scale + bias)
        top = row_max(scores)
        total, mixed = 0.0, 0.0
        for score, (_, value) in zip(scores, blocks):
            weight = jnp.exp2(score - top)
            total = total + jnp.sum(weight, axis=1, keepdims=True)
            mixed = mixed + jnp.dot(
                weight.astype(jnp.bfloat16),
                value[:, first:last],
                preferred_element_type=jnp.float32,
            )
        mixed = jnp.where(mask, mixed, 0.0)
        max_ref[:, head : head + 1] = top
        sum_ref[:, head : head + 1] = total
        for at in range(first, last, LANES):
            part = mixed[:, at - first : at - first + LANES]
            if at < done:
                acc_ref[:, at : at + LANES] += part
            else:
                acc_ref[:, at : at + LANES] = part
                done = at + LANES


def layout_attention(band, counts, queries, blocks):
    tokens, width = queries.shape
    rows = tokens // CHUNKS
    slots = blocks[0].shape[0]
    smem = pl.BlockSpec(memory_space=pltpu.SMEM)
    row = pl.BlockSpec((rows, width), lambda i: (i, 0))
    stat = pl.BlockSpec((rows, LANES), lambda i: (i, 0))
    operands, specs = [], []
    for block in blocks:
        operands += [block, block]
        specs += [
            pl.BlockSpec((slots, width), lambda i: (0, 0)),
            pl.BlockSpec((slots, width), lambda i: (0, 1)),
        ]
    return pl.pallas_call(
        layout_kernel,
        grid=(CHUNKS,),
        in_specs=[smem, smem, row] + specs,
        out_specs=[row, stat, stat],
        out_shape=[
            jax.ShapeDtypeStruct((tokens, width), jnp.float32),
            jax.ShapeDtypeStruct((tokens, LANES), jnp.float32),
            jax.ShapeDtypeStruct((tokens, LANES), jnp.float32),
        ],
        compiler_params=pltpu.CompilerParams(vmem_limit_bytes=VMEM_LIMIT),
        name="layout_attention",
    )(band, counts, queries, *operands)


def view_kernel(
    half, shared_ref, q_ref, hidden_ref, acc_ref, max_ref, sum_ref,
    left_key, left_value, right_key, right_value, out_ref, mixed_ref,
):
    rows, width = q_ref.shape
    scale = LOG2E / math.sqrt(width // HEADS)
    count = left_key.shape[0]
    column = lax.rem(lane_index(count), half)
    left_bias = jnp.where(column >= half - shared_ref[0, 0], 0.0, DEAD)
    right_bias = jnp.where(column < shared_ref[0, 1], 0.0, DEAD)
    done = 0
    for head in range(HEADS):
        low, high, first, last = head_span(head, width)
        mask = head_mask(head, rows, width)
        query = jnp.where(mask, q_ref[:, first:last], jnp.bfloat16(0))
        scores = []
        for key, bias in ((left_key, left_bias), (right_key, right_bias)):
            product = lax.dot_general(
                query, key[:, first:last], NT, preferred_element_type=jnp.float32
            )
            scores.append(product * scale + bias)
        before = max_ref[:, head : head + 1]
        top = jnp.maximum(row_max(scores), before)
        carry = jnp.exp2(before - top)
        total = sum_ref[:, head : head + 1] * carry
        mixed = acc_ref[:, first:last] * carry
        for score, value in zip(scores, (left_value, right_value)):
            weight = jnp.exp2(score - top)
            total = total + jnp.sum(weight, axis=1, keepdims=True)
            mixed = mixed + jnp.dot(
                weight.astype(jnp.bfloat16),
                value[:, first:last],
                preferred_element_type=jnp.float32,
            )
        mixed = jnp.where(mask, mixed * (1.0 / total), 0.0)
        for at in range(first, last, LANES):
            part = mixed[:, at - first : at - first + LANES]
            if at < done:
                mixed_ref[:, at : at + LANES] += part
            else:
                mixed_ref[:, at : at + LANES] = part
                done = at + LANES
    out_ref[...] = (hidden_ref[...].astype(jnp.float32) + mixed_ref[...]).astype(jnp.bfloat16)


def view_attention(chunk, half, shared, queries, hidden, partial, left, right):
    tokens, width = queries.shape
    rows = tokens // CHUNKS
    keys = left.shape[0]
    row = pl.BlockSpec((rows, width), lambda i: (chunk, 0))
    stat = pl.BlockSpec((rows, LANES), lambda i: (chunk, 0))
    key_spec = pl.BlockSpec((keys, width), lambda i: (0, 0))
    value_spec = pl.BlockSpec((keys, width), lambda i: (0, 1))
    return pl.pallas_call(
        functools.partial(view_kernel, half),
        grid=(1,),
        in_specs=[
            pl.BlockSpec(memory_space=pltpu.SMEM), row, row, row, stat, stat,
            key_spec, value_spec, key_spec, value_spec,
        ],
        out_specs=pl.BlockSpec((rows, width), lambda i: (0, 0)),
        out_shape=jax.ShapeDtypeStruct((rows, width), jnp.bfloat16),
        scratch_shapes=[pltpu.VMEM((rows, width), jnp.float32)],
        compiler_params=pltpu.CompilerParams(vmem_limit_bytes=VMEM_LIMIT),
        name="view_attention",
    )(shared, queries, hidden, *partial, left, left, right, right)


def temporal_kernel(x_ref, gain_ref, w_ref, out_ref, normed_ref, qkv_ref):
    frames, group, width = x_ref.shape
    rows = frames * group
    scale = LOG2E / math.sqrt(width // HEADS)
    state = x_ref[...].reshape(rows, width).astype(jnp.float32)
    inverse = lax.rsqrt(jnp.mean(state * state, axis=1, keepdims=True) + EPSILON)
    normed_ref[...] = (state * inverse * gain_ref[...]).astype(jnp.bfloat16)
    step = 3 * LANES
    for at in range(0, 3 * width, step):
        qkv_ref[:, at : at + step] = jnp.dot(
            normed_ref[...], w_ref[:, at : at + step], preferred_element_type=jnp.float32
        ).astype(jnp.bfloat16)
    row = lax.broadcasted_iota(jnp.int32, (rows, rows), 0)
    column = lax.broadcasted_iota(jnp.int32, (rows, rows), 1)
    bias = jnp.where(lax.rem(row, group) == lax.rem(column, group), 0.0, DEAD)
    tiles = {}
    for head in range(HEADS):
        low, high, first, last = head_span(head, width)
        mask = head_mask(head, rows, width)
        query = jnp.where(mask, qkv_ref[:, first:last], jnp.bfloat16(0))
        key = qkv_ref[:, width + first : width + last]
        value = qkv_ref[:, 2 * width + first : 2 * width + last]
        score = lax.dot_general(query, key, NT, preferred_element_type=jnp.float32)
        score = score * scale + bias
        weight = jnp.exp2(score - jnp.max(score, axis=1, keepdims=True))
        total = jnp.sum(weight, axis=1, keepdims=True)
        mixed = jnp.dot(weight.astype(jnp.bfloat16), value, preferred_element_type=jnp.float32)
        mixed = jnp.where(mask, mixed * (1.0 / total), 0.0)
        for at in range(first, last, LANES):
            part = mixed[:, at - first : at - first + LANES]
            tiles[at] = tiles[at] + part if at in tiles else part
            if high >= at + LANES:
                out_ref[:, :, at : at + LANES] = (
                    tiles.pop(at).astype(jnp.bfloat16).reshape(frames, group, LANES)
                )


def temporal_attention(regrouped, norm_gain, w_qkv):
    frames, group, width = regrouped.shape
    rows = frames * group
    return pl.pallas_call(
        temporal_kernel,
        out_shape=jax.ShapeDtypeStruct(regrouped.shape, jnp.bfloat16),
        scratch_shapes=[
            pltpu.VMEM((rows, width), jnp.bfloat16),
            pltpu.VMEM((rows, 3 * width), jnp.bfloat16),
        ],
        compiler_params=pltpu.CompilerParams(vmem_limit_bytes=VMEM_LIMIT),
        name="temporal_attention",
    )(regrouped, norm_gain.reshape(1, width), w_qkv)


def exchange(array, axis, flip):
    length = lax.axis_size(axis)
    return lax.ppermute(array, axis, [(i, i ^ flip) for i in range(length)])


def passed_along(array, axis, by):
    length = lax.axis_size(axis)
    return lax.ppermute(array, axis, [(i, (i + by) % length) for i in range(length)])


def regroup(array):
    return lax.all_to_all(array, "frame", split_axis=0, concat_axis=0, tiled=True)


def per_device(
    hidden, cond_queries, cond_kv, layout_kv, layout_count, intersection, norm_gain, w_qkv
):
    patch_rows, patch_cols, width = hidden.shape[2:]
    half = patch_cols // 2
    tokens = patch_rows * patch_cols
    frames = lax.axis_size("frame")
    own = cond_kv[0, 0]
    left = passed_along(own[:, half:, :], "view", 1).reshape(patch_rows * half, 2 * width)
    right = passed_along(own[:, :half, :], "view", -1).reshape(patch_rows * half, 2 * width)
    layout = layout_kv[0]
    across = exchange(layout, "band", 2)
    beside = exchange(layout, "band", 1)
    diagonal = exchange(across, "band", 1)
    band = lax.axis_index("band").reshape(1)
    queries = cond_queries[0, 0].reshape(tokens, width)
    hidden_rows = hidden[0, 0].reshape(tokens, width)
    partial = layout_attention(
        band, layout_count, queries, [layout, beside, across, diagonal]
    )
    outputs = []
    for chunk in range(CHUNKS):
        state = view_attention(
            chunk, half, intersection, queries, hidden_rows, partial, left, right
        )
        regrouped = regroup(state.reshape(frames, -1, width))
        outputs.append(regroup(temporal_attention(regrouped, norm_gain, w_qkv)))
    rows = [output.reshape(tokens // CHUNKS, width) for output in outputs]
    return jnp.concatenate(rows, axis=0).reshape(1, 1, patch_rows, patch_cols, width)


def solution(mesh):
    in_specs = (
        P("view", "frame", "band", None, None),
        P("view", "frame", "band", None, None),
        P("view", "frame", "band", None, None),
        P("frame", "band", None),
        P("frame", None),
        P("view", None),
        P(),
        P(),
    )
    out_specs = P("view", "frame", "band", None, None)
    return jax.shard_map(
        per_device, mesh=mesh, in_specs=in_specs, out_specs=out_specs, check_vma=False
    )
```

time: 301 us -> 149 us (0.50)
  the two profiles are of different devices: /device:TPU:8 before, /device:TPU:16 now
where the time goes in v1:
time: 149 us; the launch traced here: 148 us
  Pallas kernels  56.4 us (38%)
  waiting for transfers between devices  35.7 us (24%)
  blocking collectives  25 us (17%)
  starting transfers between devices  24.6 us (17%)
  local copies, waits for them, and re-layouts  5.23 us (4%)
    all_to_all x1, blocking collectives, regroup(): lax.all_to_all(array, 'frame', split_axis=0, concat_axis=0, tiled=True)  25 us
    all_to_all x3, waiting for transfers between devices, regroup(): lax.all_to_all(array, 'frame', split_axis=0, concat_axis=0, tiled=True)  25 us
    pallas_call x2, Pallas kernels, view_attention(): pl.pallas_call(functools.partial(view_kernel, half), grid=(1,), in_specs=...  23.1 us
    all_to_all x3, starting transfers between devices, regroup(): lax.all_to_all(array, 'frame', split_axis=0, concat_axis=0, tiled=True)  21 us
    pallas_call x2, Pallas kernels, temporal_attention(): pl.pallas_call(temporal_kernel, out_shape=jax.ShapeDtypeStruct(regrouped....  18.2 us
    pallas_call x1, Pallas kernels, layout_attention(): pl.pallas_call(layout_kernel, grid=(CHUNKS,), in_specs=[smem, smem, row]...  15.1 us
    ppermute x3, waiting for transfers between devices, exchange(): return lax.ppermute(array, axis, [(i, i ^ flip) for i in range(length)])  10.6 us
    slice x1, local copies, waits for them, and re-layouts, per_device(): own[:, :half, :]  3.27 us
  transfers between devices with their start and end apart: 8, of which 5 were waited for; matrix products, arithmetic and copies ran while one was open for 3% of the time, Pallas kernels for 30%

profile of v1, /device:TPU:16, one launch (start us, length us, event | category | flops | bytes accessed | tf_op | source)
XLA Modules:
  0.0 148.1 jit_solution(13308203292412189760)
XLA Ops:
  0.0 1.5 %collective-permute-start.1 = (bf16[128,2304]{1,0:T(8,128)(2,1)}, bf16[128,2304]{1,0:T(8,128)(2,1)S(1)}, u32[]{:S(2)}, u32[]{:S(2)}) collective-permute-start(bf16[128,2304]{1,0:T(8,128)(2,1)} %bitcast.25), channel_id=1, source_target_pairs={{0,2},{1,3},{2,0},{3,1},{4,6},{5,7},{6,4},{7,5},{8,10},{9,11},{10,... | collective-permute-start | bytes 1769480 | tf_op jit(solution)/shard_map/ppermute | solution.py:238
  1.5 3.3 %fusion = (bf16[8,32,2304]{2,1,0:T(8,128)(2,1)}, bf16[8,32,2304]{2,1,0:T(8,128)(2,1)}) fusion(bf16[8,64,2304]{2,1,0:T(8,128)(2,1)} %bitcast.29), kind=kLoop, calls=%fused_computation.1 | loop fusion | bytes 4718592 | tf_op jit(solution)/shard_map/slice | solution.py:259
  4.8 0.4 collective-permute-start.4
  5.2 1.6 %collective-permute-start.3 = (bf16[8,32,2304]{2,1,0:T(8,128)(2,1)}, bf16[8,32,2304]{2,1,0:T(8,128)(2,1)S(1)}, u32[]{:S(2)}, u32[]{:S(2)}) collective-permute-start(bf16[8,32,2304]{2,1,0:T(8,128)(2,1)} %get-tuple-element.12), channel_id=1, source_target_pairs={{0,64},{64,128},{128,192},{192,0},{1,65},{65,129},{129,193},{193,1... | collective-permute-start | bytes 3538952 | tf_op jit(solution)/shard_map/ppermute | solution.py:243
  6.8 0.0 collective-permute-start
  6.8 8.5 %collective-permute-done.1.refs_4_.refs_5_ = bf16[128,2304]{1,0:T(8,128)(2,1)S(1)} collective-permute-done((bf16[128,2304]{1,0:T(8,128)(2,1)}, bf16[128,2304]{1,0:T(8,128)(2,1)S(1)}, u32[]{:S(2)}, u32[]{:S(2)}) %collective-permute-start.1) | collective-permute-done | bytes 589856 | tf_op jit(solution)/shard_map/ppermute | solution.py:238
  15.3 2.1 %collective-permute-done.2.refs_6_.refs_7_ = bf16[128,2304]{1,0:T(8,128)(2,1)} collective-permute-done((bf16[128,2304]{1,0:T(8,128)(2,1)S(1)}, bf16[128,2304]{1,0:T(8,128)(2,1)}, u32[]{:S(2)}, u32[]{:S(2)}) %collective-permute-start.2) | collective-permute-done | bytes 589856 | tf_op jit(solution)/shard_map/ppermute | solution.py:238
  17.4 15.1 %layout_attention.1 = (f32[512,1152]{1,0:T(8,128)}, f32[512,128]{1,0:T(8,128)}, f32[512,128]{1,0:T(8,128)}) custom-call(s32[1]{0:T(128)} %bitcast.2.band_ref, s32[1,4]{1,0:T(1,128)} %count_ref.1, bf16[512,1152]{1,0:T(8,128)(2,1)} %bitcast.20, bf16[128,2304]{1,0:T(8,128)(2,1)} %bitcast.26, bf16[128,2304]{1,0:T(8,128)(2,1)} %bitcast.27, ...), custom_call_target="tpu_custom_call" | custom-call | tf_op jit(solution)/shard_map/layout_attention/pallas_call | solution.py:101
  32.5 0.0 collective-permute-done.3
  32.6 1.0 copy-done
  33.5 0.4 copy-done.1
  33.9 11.5 %view_attention.3 = bf16[256,1152]{1,0:T(8,128)(2,1)} custom-call(s32[1,2]{1,0:T(1,128)} %shared_ref.3, bf16[512,1152]{1,0:T(8,128)(2,1)} %bitcast.21, bf16[512,1152]{1,0:T(8,128)(2,1)} %bitcast.23, f32[512,1152]{1,0:T(8,128)} %get-tuple-element.8.acc_ref, f32[512,128]{1,0:T(8,128)} %get-tuple-element.9.max_ref, f32[512,128]{1,0:T(8,128)} %get-tuple-element.10.sum_ref, ...), custom_call_target="tpu_custom_call" | custom-call | tf_op jit(solution)/shard_map/view_attention/pallas_call | solution.py:169
  45.5 11.0 %all-to-all-start.2 = ((bf16[16,16,1152]{2,1,0:T(8,128)(2,1)}), bf16[16,16,1152]{2,1,0:T(8,128)(2,1)S(1)}, u32[]{:S(2)}, u32[]{:S(2)}) async-start(bf16[16,16,1152]{2,1,0:T(8,128)(2,1)} %bitcast.33), calls=%async_computation.2 | async-start | bytes 1179648 | tf_op jit(solution)/shard_map/all_to_all | solution.py:247
  56.5 11.5 %view_attention.2 = bf16[256,1152]{1,0:T(8,128)(2,1)} custom-call(s32[1,2]{1,0:T(1,128)} %shared_ref.3, bf16[512,1152]{1,0:T(8,128)(2,1)} %bitcast.22, bf16[512,1152]{1,0:T(8,128)(2,1)} %bitcast.24, f32[512,1152]{1,0:T(8,128)} %get-tuple-element.8.acc_ref, f32[512,128]{1,0:T(8,128)} %get-tuple-element.9.max_ref, f32[512,128]{1,0:T(8,128)} %get-tuple-element.10.sum_ref, ...), custom_call_target="tpu_custom_call" | custom-call | tf_op jit(solution)/shard_map/view_attention/pallas_call | solution.py:169
  68.0 7.0 %all-to-all-done.2.x_ref = bf16[16,16,1152]{2,1,0:T(8,128)(2,1)S(1)} async-done(((bf16[16,16,1152]{2,1,0:T(8,128)(2,1)}), bf16[16,16,1152]{2,1,0:T(8,128)(2,1)S(1)}, u32[]{:S(2)}, u32[]{:S(2)}) %all-to-all-start.2) | async-done | bytes 589856 | tf_op jit(solution)/shard_map/all_to_all | solution.py:247
  75.0 4.9 %all-to-all-start = ((bf16[16,16,1152]{2,1,0:T(8,128)(2,1)}), bf16[16,16,1152]{2,1,0:T(8,128)(2,1)S(1)}, u32[]{:S(2)}, u32[]{:S(2)}) async-start(bf16[16,16,1152]{2,1,0:T(8,128)(2,1)} %bitcast.32), calls=%async_computation | async-start | bytes 1179648 | tf_op jit(solution)/shard_map/all_to_all | solution.py:247
  80.0 0.6 reshape.32.gain_ref
  80.6 9.1 %temporal_attention.3 = bf16[16,16,1152]{2,1,0:T(8,128)(2,1)} custom-call(bf16[16,16,1152]{2,1,0:T(8,128)(2,1)} %copy-done.4, f32[1,1152]{1,0:T(1,128)} %reshape.32.gain_ref, bf16[1152,3456]{1,0:T(8,128)(2,1)} %w_ref.3), custom_call_target="tpu_custom_call" | custom-call | tf_op jit(solution)/shard_map/temporal_attention/pallas_call | solution.py:224
  89.7 8.7 %all-to-all-done.x_ref = bf16[16,16,1152]{2,1,0:T(8,128)(2,1)S(1)} async-done(((bf16[16,16,1152]{2,1,0:T(8,128)(2,1)}), bf16[16,16,1152]{2,1,0:T(8,128)(2,1)S(1)}, u32[]{:S(2)}, u32[]{:S(2)}) %all-to-all-start) | async-done | bytes 589856 | tf_op jit(solution)/shard_map/all_to_all | solution.py:247
  98.4 5.1 %all-to-all-start.3 = ((bf16[16,16,1152]{2,1,0:T(8,128)(2,1)}), bf16[16,16,1152]{2,1,0:T(8,128)(2,1)S(1)}, u32[]{:S(2)}, u32[]{:S(2)}) async-start(bf16[16,16,1152]{2,1,0:T(8,128)(2,1)} %temporal_attention.3), calls=%async_computation.3 | async-start | bytes 1179648 | tf_op jit(solution)/shard_map/all_to_all | solution.py:247
  103.5 9.1 %temporal_attention.2 = bf16[16,16,1152]{2,1,0:T(8,128)(2,1)} custom-call(bf16[16,16,1152]{2,1,0:T(8,128)(2,1)} %copy-done.5, f32[1,1152]{1,0:T(1,128)} %reshape.32.gain_ref, bf16[1152,3456]{1,0:T(8,128)(2,1)} %w_ref.3), custom_call_target="tpu_custom_call" | custom-call | tf_op jit(solution)/shard_map/temporal_attention/pallas_call | solution.py:224
  112.7 9.3 %all-to-all-done.3 = bf16[16,16,1152]{2,1,0:T(8,128)(2,1)S(1)} async-done(((bf16[16,16,1152]{2,1,0:T(8,128)(2,1)}), bf16[16,16,1152]{2,1,0:T(8,128)(2,1)S(1)}, u32[]{:S(2)}, u32[]{:S(2)}) %all-to-all-start.3) | async-done | bytes 589856 | tf_op jit(solution)/shard_map/all_to_all | solution.py:247
  121.9 25.0 %all_to_all.20 = bf16[16,16,1152]{2,1,0:T(8,128)(2,1)S(1)} all-to-all(bf16[16,16,1152]{2,1,0:T(8,128)(2,1)} %temporal_attention.2), channel_id=1, replica_groups=mesh['view'=4,'frame'=16,'band'=4] {'frame'}, dimensions={0} | all-to-all | bytes 1179648 | tf_op jit(solution)/shard_map/all_to_all | solution.py:247
  147.0 1.1 pad_maximum_fusion
  (15 shorter events, 0.0 us)
Async XLA Ops:
  0.0 15.3 %collective-permute-start.1 = (bf16[128,2304]{1,0:T(8,128)(2,1)}, bf16[128,2304]{1,0:T(8,128)(2,1)S(1)}, u32[]{:S(2)}, u32[]{:S(2)}) collective-permute-start(bf16[128,2304]{1,0:T(8,128)(2,1)} %bitcast.25), channel_id=1, source_target_pairs={{0,2},{1,3},{2,0},{3,1},{4,6},{5,7},{6,4},{7,5},{8,10},{9,11},{10,... | collective-permute-start | bytes 1769480 | tf_op jit(solution)/shard_map/ppermute | solution.py:238
  1.5 5.3 %copy-start.2 = (bf16[1,128,2304]{2,1,0:T(8,128)(2,1)S(1)}, bf16[1,128,2304]{2,1,0:T(8,128)(2,1)}, u32[]{:S(2)}) copy-start(bf16[1,128,2304]{2,1,0:T(8,128)(2,1)} %param.11) | copy-start | bytes 1769476
  4.8 27.7 %collective-permute-start.4 = (bf16[8,32,2304]{2,1,0:T(8,128)(2,1)}, bf16[8,32,2304]{2,1,0:T(8,128)(2,1)S(1)}, u32[]{:S(2)}, u32[]{:S(2)}) collective-permute-start(bf16[8,32,2304]{2,1,0:T(8,128)(2,1)} %get-tuple-element.11), channel_id=1, source_target_pairs={{0,192},{64,0},{128,64},{192,128},{1,193},{65,1},{129,65},{193,129... | collective-permute-start | bytes 3538952 | tf_op jit(solution)/shard_map/ppermute | solution.py:243
  5.2 27.4 %collective-permute-start.3 = (bf16[8,32,2304]{2,1,0:T(8,128)(2,1)}, bf16[8,32,2304]{2,1,0:T(8,128)(2,1)S(1)}, u32[]{:S(2)}, u32[]{:S(2)}) collective-permute-start(bf16[8,32,2304]{2,1,0:T(8,128)(2,1)} %get-tuple-element.12), channel_id=1, source_target_pairs={{0,64},{64,128},{128,192},{192,0},{1,65},{65,129},{129,193},{193,1... | collective-permute-start | bytes 3538952 | tf_op jit(solution)/shard_map/ppermute | solution.py:243
  6.8 8.5 %collective-permute-start = (bf16[128,2304]{1,0:T(8,128)(2,1)S(1)}, bf16[128,2304]{1,0:T(8,128)(2,1)}, u32[]{:S(2)}, u32[]{:S(2)}) collective-permute-start(bf16[128,2304]{1,0:T(8,128)(2,1)S(1)} %bitcast.28), channel_id=1, source_target_pairs={{0,1},{1,0},{2,3},{3,2},{4,5},{5,4},{6,7},{7,6},{8,9},{9,8},{10,11... | collective-permute-start | bytes 1769480 | tf_op jit(solution)/shard_map/ppermute | solution.py:238
  15.3 2.1 %copy-start.3 = (bf16[128,2304]{1,0:T(8,128)(2,1)}, bf16[128,2304]{1,0:T(8,128)(2,1)S(1)}, u32[]{:S(2)}) copy-start(bf16[128,2304]{1,0:T(8,128)(2,1)S(1)} %collective-permute-done.1.refs_4_.refs_5_) | copy-start | bytes 1769476
  15.3 2.1 %collective-permute-start.2 = (bf16[128,2304]{1,0:T(8,128)(2,1)S(1)}, bf16[128,2304]{1,0:T(8,128)(2,1)}, u32[]{:S(2)}, u32[]{:S(2)}) collective-permute-start(bf16[128,2304]{1,0:T(8,128)(2,1)S(1)} %collective-permute-done.1.refs_4_.refs_5_), channel_id=1, source_target_pairs={{0,1},{1,0},{2,3},{3,2},{4,5},{5,4},{6,7},{7,6},{8,9},{9,8},{10,11... | collective-permute-start | bytes 1769480 | tf_op jit(solution)/shard_map/ppermute | solution.py:238
  32.5 1.0 copy-start
  32.6 1.3 copy-start.1
  45.5 29.6 %all-to-all-start.2 = ((bf16[16,16,1152]{2,1,0:T(8,128)(2,1)}), bf16[16,16,1152]{2,1,0:T(8,128)(2,1)S(1)}, u32[]{:S(2)}, u32[]{:S(2)}) async-start(bf16[16,16,1152]{2,1,0:T(8,128)(2,1)} %bitcast.33), calls=%async_computation.2 | async-start | bytes 1179648 | tf_op jit(solution)/shard_map/all_to_all | solution.py:247
  68.0 11.9 %copy-start.6 = (f32[1152]{0:T(1024)S(1)}, f32[1152]{0:T(1024)}, u32[]{:S(2)}) copy-start(f32[1152]{0:T(1024)} %param.14) | copy-start | bytes 13828
  75.0 5.5 %copy-start.4 = (bf16[16,16,1152]{2,1,0:T(8,128)(2,1)}, bf16[16,16,1152]{2,1,0:T(8,128)(2,1)S(1)}, u32[]{:S(2)}) copy-start(bf16[16,16,1152]{2,1,0:T(8,128)(2,1)S(1)} %all-to-all-done.2.x_ref) | copy-start | bytes 1769476
  75.0 23.4 %all-to-all-start = ((bf16[16,16,1152]{2,1,0:T(8,128)(2,1)}), bf16[16,16,1152]{2,1,0:T(8,128)(2,1)S(1)}, u32[]{:S(2)}, u32[]{:S(2)}) async-start(bf16[16,16,1152]{2,1,0:T(8,128)(2,1)} %bitcast.32), calls=%async_computation | async-start | bytes 1179648 | tf_op jit(solution)/shard_map/all_to_all | solution.py:247
  98.4 5.1 %copy-start.5 = (bf16[16,16,1152]{2,1,0:T(8,128)(2,1)}, bf16[16,16,1152]{2,1,0:T(8,128)(2,1)S(1)}, u32[]{:S(2)}) copy-start(bf16[16,16,1152]{2,1,0:T(8,128)(2,1)S(1)} %all-to-all-done.x_ref) | copy-start | bytes 1769476
  98.4 23.5 %all-to-all-start.3 = ((bf16[16,16,1152]{2,1,0:T(8,128)(2,1)}), bf16[16,16,1152]{2,1,0:T(8,128)(2,1)S(1)}, u32[]{:S(2)}, u32[]{:S(2)}) async-start(bf16[16,16,1152]{2,1,0:T(8,128)(2,1)} %temporal_attention.3), calls=%async_computation.3 | async-start | bytes 1179648 | tf_op jit(solution)/shard_map/all_to_all | solution.py:247

commit v2 on v0

v2 whole, which is shorter than its diff:
```python
import functools
import math

import jax
import jax.numpy as jnp
from jax import lax
from jax.experimental import pallas as pl
from jax.experimental.pallas import tpu as pltpu
from jax.sharding import PartitionSpec as P

HEADS = 16
LANES = 128
HEAD_STEPS = (0, 6, 11, 16)
QUERY_ROWS = 256
EPSILON = 1e-06
DEAD = -1e30
VMEM_LIMIT = 32 << 20
LOG2E = 1.4426950408889634
NT = (((1,), (1,)), ((), ()))


def head_span(head, width):
    size = width // HEADS
    low, high = head * size, (head + 1) * size
    return low, high, low // LANES * LANES, -(-high // LANES) * LANES


def head_mask(head, rows, width):
    low, high, first, last = head_span(head, width)
    column = lax.broadcasted_iota(jnp.int32, (rows, last - first), 1) + first
    return (column >= low) & (column < high)


def lane_index(count):
    return lax.broadcasted_iota(jnp.int32, (1, count), 1)


def over_lanes(reduce_lanes, combine, pieces):
    tiles = [
        piece[:, at : at + LANES] for piece in pieces for at in range(0, piece.shape[1], LANES)
    ]
    while len(tiles) > 1:
        pairs = [combine(a, b) for a, b in zip(tiles[0::2], tiles[1::2])]
        tiles = pairs + tiles[len(tiles) // 2 * 2 :]
    return reduce_lanes(tiles[0], axis=1, keepdims=True)


def column_cuts(width):
    return (0, *(head_span(end - 1, width)[3] for end in HEAD_STEPS[1:]))


def cond_kernel(half, width, heads, cuts, count_kv, *refs):
    count_ref, shared_ref, q_ref, hidden_ref = refs[:4]
    layout_refs = refs[4:8]
    kv_refs = refs[8 : 8 + 2 * count_kv]
    rest = list(refs[8 + 2 * count_kv :])
    mixed_ref, key_ref, value_ref, sems = rest[-4:]
    last_step = heads[1] == HEADS
    finished = []
    if last_step:
        finished, rest = rest[: count_kv - 1], rest[count_kv - 1 :]
    carry_ref = rest.pop(0) if heads[0] > 0 else None
    out_ref = rest[0]
    rows = q_ref.shape[0]
    scale = LOG2E / math.sqrt(width // HEADS)
    begin = head_span(heads[0], width)[2]
    finish = head_span(heads[1] - 1, width)[3]
    keys = kv_refs[0].shape[0]
    slots = layout_refs[0].shape[0]

    @pl.when(pl.program_id(0) == 0)
    def _():
        moves = []
        for part in range(count_kv):
            start, end = max(cuts[part], begin), min(cuts[part + 1], finish)
            size = cuts[part + 1] - cuts[part]
            for side in range(2 if start < end else 0):
                low = start - cuts[part]
                moves.append((kv_refs[2 * part + side], low, size + low, side * keys, start, end))
        for block, ref in enumerate(layout_refs):
            at = 2 * keys + block * slots
            moves.append((ref, begin, width + begin, at, begin, finish))
        copies = []
        for which, target in enumerate((key_ref, value_ref)):
            for move in moves:
                ref, at, start, end = move[0], move[3], move[4], move[5]
                low = move[1 + which]
                copies.append(
                    pltpu.make_async_copy(
                        ref.at[:, low : low + end - start],
                        target.at[at : at + ref.shape[0], start - begin : end - begin],
                        sems.at[len(copies)],
                    )
                )
        for copy in copies:
            copy.start()
        for copy in copies:
            copy.wait()

    band = lax.axis_index("band")
    column = lax.rem(lane_index(keys), half)
    live = [column >= half - shared_ref[0, 0], column < shared_ref[0, 1]]
    for block in range(len(layout_refs)):
        limit = count_ref[0, jnp.bitwise_xor(band, block)]
        live.append(lane_index(slots) < limit)
    bias = jnp.concatenate([jnp.where(mask, 0.0, DEAD) for mask in live], axis=1)

    def scores_of(head):
        low, high, first, last = head_span(head, width)
        query = jnp.where(head_mask(head, rows, width), q_ref[:, first:last], jnp.bfloat16(0))
        product = lax.dot_general(
            query, key_ref[:, first - begin : last - begin], NT,
            preferred_element_type=jnp.float32,
        )
        return product * scale + bias

    done = begin
    if carry_ref is not None:
        mixed_ref[:, 0:LANES] = carry_ref[...]
        done = begin + LANES
    scores = scores_of(heads[0])
    for head in range(*heads):
        following = scores_of(head + 1) if head + 1 < heads[1] else None
        low, high, first, last = head_span(head, width)
        weights = jnp.exp2(scores - over_lanes(jnp.max, jnp.maximum, [scores]))
        total = over_lanes(jnp.sum, jnp.add, [weights])
        mixed = jnp.dot(
            weights.astype(jnp.bfloat16), value_ref[:, first - begin : last - begin],
            preferred_element_type=jnp.float32,
        )
        mixed = jnp.where(head_mask(head, rows, width), mixed * (1.0 / total), 0.0)
        for at in range(first, last, LANES):
            part = mixed[:, at - first : at - first + LANES]
            if at < done:
                mixed_ref[:, at - begin : at - begin + LANES] += part
            else:
                mixed_ref[:, at - begin : at - begin + LANES] = part
                done = at + LANES
        scores = following
    at = 0
    for ref in finished:
        out_ref[:, at : at + ref.shape[1]] = ref[...]
        at += ref.shape[1]
    size = out_ref.shape[1] - at
    out_ref[:, at:] = (
        hidden_ref[:, begin : begin + size].astype(jnp.float32) + mixed_ref[:, :size]
    ).astype(jnp.bfloat16)
    if not last_step:
        rest[1][...] = mixed_ref[:, size : size + LANES]


def cond_attention(half, step, scalars, queries, hidden, layout, kv_parts, finished, carry):
    tokens, width = queries.shape
    heads = HEAD_STEPS[step], HEAD_STEPS[step + 1]
    cuts = column_cuts(width)
    last_step = heads[1] == HEADS
    begin = head_span(heads[0], width)[2]
    read = head_span(heads[1] - 1, width)[3]
    size = width if last_step else heads[1] * (width // HEADS) // LANES * LANES - begin
    smem = pl.BlockSpec(memory_space=pltpu.SMEM)

    def rows_of(columns):
        return pl.BlockSpec((QUERY_ROWS, columns), lambda i: (i, 0))

    flat = [array for pair in kv_parts for array in pair]
    operands = [*scalars, queries, hidden, *layout, *flat]
    specs = [smem, smem, rows_of(read), rows_of(read)]
    specs += [pl.BlockSpec(memory_space=pltpu.VMEM) for _ in (*layout, *flat)]
    keys = 2 * flat[0].shape[0] + len(layout) * layout[0].shape[0]
    copies = 2 * (len(layout) + len(flat))
    if last_step:
        operands += finished
        specs += [rows_of(array.shape[1]) for array in finished]
    if carry is not None:
        operands.append(carry)
        specs.append(rows_of(LANES))
    out_specs = [rows_of(size)]
    out_shape = [jax.ShapeDtypeStruct((tokens, size), jnp.bfloat16)]
    if last_step:
        out_shape = [pltpu.HBM((tokens, size), jnp.bfloat16)]
    else:
        out_specs.append(rows_of(LANES))
        out_shape.append(jax.ShapeDtypeStruct((tokens, LANES), jnp.float32))
    return pl.pallas_call(
        functools.partial(cond_kernel, half, width, heads, cuts, len(kv_parts)),
        grid=(tokens // QUERY_ROWS,),
        in_specs=specs,
        out_specs=out_specs,
        out_shape=out_shape,
        scratch_shapes=[
            pltpu.VMEM((QUERY_ROWS, read - begin), jnp.float32),
            pltpu.VMEM((keys, read - begin), jnp.bfloat16),
            pltpu.VMEM((keys, read - begin), jnp.bfloat16),
            pltpu.SemaphoreType.DMA((copies,)),
        ],
        compiler_params=pltpu.CompilerParams(vmem_limit_bytes=VMEM_LIMIT),
        name="cond_attention",
    )(*operands)


def temporal_kernel(
    x_ref, gain_ref, w_ref, out_ref, normed_ref, qkv_ref
):
    frames, positions, width = out_ref.shape
    group = 16
    rows = frames * group
    scale = LOG2E / math.sqrt(width // HEADS)
    step = pl.program_id(0)

    @pl.when(step == 0)
    def _():
        for at in range(0, positions, group):
            state = x_ref[:, at : at + group, :].reshape(rows, width).astype(jnp.float32)
            inverse = lax.rsqrt(jnp.mean(state * state, axis=1, keepdims=True) + EPSILON)
            normed_ref[at * frames : at * frames + rows, :] = (
                state * inverse * gain_ref[...]
            ).astype(jnp.bfloat16)

    for part in range(3):

        @pl.when(step == part)
        def _():
            qkv_ref[:, part * width : (part + 1) * width] = jnp.dot(
                normed_ref[...], w_ref[...], preferred_element_type=jnp.float32
            ).astype(jnp.bfloat16)

    @pl.when(step == 2)
    def _():
        row = lax.broadcasted_iota(jnp.int32, (rows, rows), 0)
        column = lax.broadcasted_iota(jnp.int32, (rows, rows), 1)
        bias = jnp.where(lax.rem(row, group) == lax.rem(column, group), 0.0, DEAD)
        for at in range(0, positions, group):
            span = slice(at * frames, at * frames + rows)
            tiles = {}
            for head in range(HEADS):
                low, high, first, last = head_span(head, width)
                mask = head_mask(head, rows, width)
                query = jnp.where(mask, qkv_ref[span, first:last], jnp.bfloat16(0))
                key = qkv_ref[span, width + first : width + last]
                value = qkv_ref[span, 2 * width + first : 2 * width + last]
                score = lax.dot_general(query, key, NT, preferred_element_type=jnp.float32)
                score = score * scale + bias
                weight = jnp.exp2(score - over_lanes(jnp.max, jnp.maximum, [score]))
                total = over_lanes(jnp.sum, jnp.add, [weight])
                mixed = jnp.dot(
                    weight.astype(jnp.bfloat16), value, preferred_element_type=jnp.float32
                )
                mixed = jnp.where(mask, mixed * (1.0 / total), 0.0)
                for tile in range(first, last, LANES):
                    part = mixed[:, tile - first : tile - first + LANES]
                    tiles[tile] = tiles[tile] + part if tile in tiles else part
                    if high >= tile + LANES:
                        out_ref[:, at : at + group, tile : tile + LANES] = (
                            tiles.pop(tile).astype(jnp.bfloat16).reshape(frames, group, LANES)
                        )


def temporal_attention(regrouped, norm_gain, w_qkv):
    frames, positions, width = regrouped.shape
    whole = pl.BlockSpec(regrouped.shape, lambda i: (0, 0, 0))
    return pl.pallas_call(
        temporal_kernel,
        grid=(3,),
        in_specs=[
            whole,
            pl.BlockSpec((1, width), lambda i: (0, 0)),
            pl.BlockSpec((width, width), lambda i: (0, i)),
        ],
        out_specs=whole,
        out_shape=jax.ShapeDtypeStruct((frames, positions, width), jnp.bfloat16),
        scratch_shapes=[
            pltpu.VMEM((frames * positions, width), jnp.bfloat16),
            pltpu.VMEM((frames * positions, 3 * width), jnp.bfloat16),
        ],
        compiler_params=pltpu.CompilerParams(vmem_limit_bytes=VMEM_LIMIT),
        name="temporal_attention",
    )(
        regrouped,
        norm_gain.reshape(1, width),
        pltpu.with_memory_space_constraint(w_qkv, pltpu.HBM),
    )


def split_kernel(half, cuts, kv_ref, *refs):
    out_refs, sems = refs[:-1], refs[-1]
    width = kv_ref.shape[2] // 2
    copies = []
    for piece, (start, end) in enumerate(zip(cuts, cuts[1:])):
        size = end - start
        for side, columns in enumerate((slice(half, 2 * half), slice(0, half))):
            out_ref = out_refs[2 * piece + side]
            for part in range(2):
                low = part * width + start
                copies.append(
                    pltpu.make_async_copy(
                        kv_ref.at[:, columns, low : low + size],
                        out_ref.at[:, :, part * size : (part + 1) * size],
                        sems.at[len(copies)],
                    )
                )
    for copy in copies:
        copy.start()
    for copy in copies:
        copy.wait()


def split_halves(own, cuts):
    rows, columns = own.shape[:2]
    shapes = [
        jax.ShapeDtypeStruct((rows, columns // 2, 2 * (end - start)), own.dtype)
        for start, end in zip(cuts, cuts[1:])
        for _ in range(2)
    ]
    local = pl.BlockSpec(memory_space=pltpu.VMEM)
    pieces = pl.pallas_call(
        functools.partial(split_kernel, columns // 2, cuts),
        in_specs=[pl.BlockSpec(memory_space=pltpu.HBM)],
        out_specs=[local] * len(shapes),
        out_shape=shapes,
        scratch_shapes=[pltpu.SemaphoreType.DMA((2 * len(shapes),))],
        compiler_params=pltpu.CompilerParams(vmem_limit_bytes=VMEM_LIMIT),
        name="split_halves",
    )(own)
    return list(zip(pieces[0::2], pieces[1::2]))


def exchange(array, axis, flip):
    length = lax.axis_size(axis)
    return lax.ppermute(array, axis, [(i, i ^ flip) for i in range(length)])


def passed_along(array, axis, by):
    length = lax.axis_size(axis)
    return lax.ppermute(array, axis, [(i, (i + by) % length) for i in range(length)])


def regroup(array):
    return lax.all_to_all(array, "frame", split_axis=0, concat_axis=0, tiled=True)


def per_device(
    hidden, cond_queries, cond_kv, layout_kv, layout_count, intersection, norm_gain, w_qkv
):
    patch_rows, patch_cols, width = hidden.shape[2:]
    half = patch_cols // 2
    tokens = patch_rows * patch_cols
    frames = lax.axis_size("frame")
    cuts = column_cuts(width)
    own = cond_kv[0, 0]

    def sent(pair):
        return tuple(
            passed_along(side, "view", by).reshape(patch_rows * half, -1)
            for side, by in zip(pair, (1, -1))
        )

    layout = layout_kv[0]
    (first_source,) = split_halves(own, cuts[:2])
    first = sent(first_source)
    across = exchange(layout, "band", 2)
    beside = exchange(layout, "band", 1)
    sources, across = lax.optimization_barrier((split_halves(own, cuts[1:]), across))
    diagonal = exchange(across, "band", 1)
    second = sent(sources[0])
    last_source, first = lax.optimization_barrier((sources[1], first))
    kv_parts = [first, second, sent(last_source)]
    layout = (layout, beside, across, diagonal)
    scalars = (layout_count, intersection)
    queries = cond_queries[0, 0].reshape(tokens, width)
    hidden_rows = hidden[0, 0].reshape(tokens, width)
    finished, carry = [], None
    for step in range(len(kv_parts)):
        result = cond_attention(
            half, step, scalars, queries, hidden_rows, layout, kv_parts[: step + 1],
            finished, carry,
        )
        finished, carry = finished + [result[0]], result[-1]
    regrouped = regroup(finished[-1].reshape(frames, -1, width))
    output = regroup(temporal_attention(regrouped, norm_gain, w_qkv))
    return output.reshape(1, 1, patch_rows, patch_cols, width)


def solution(mesh):
    in_specs = (
        P("view", "frame", "band", None, None),
        P("view", "frame", "band", None, None),
        P("view", "frame", "band", None, None),
        P("frame", "band", None),
        P("frame", None),
        P("view", None),
        P(),
        P(),
    )
    out_specs = P("view", "frame", "band", None, None)
    return jax.shard_map(
        per_device, mesh=mesh, in_specs=in_specs, out_specs=out_specs, check_vma=False
    )
```

time: 301 us -> 131 us (0.44)
  blocking collectives: 129 us -> 37.6 us
  local copies, waits for them, and re-layouts: 51.5 us -> 2.71 us
  matrix products: 46.3 us -> 0 us
  other arithmetic: 44.2 us -> 0 us
  Pallas kernels: 0 us -> 29.1 us
  waiting for transfers between devices: 13.8 us -> 41.1 us
  starting transfers between devices: 2.19 us -> 19.9 us
  between operations: 14.2 us -> 0.16 us
    all_to_all x2 -> x1, blocking collectives: 129 us -> 37.6 us  [regroup(): lax.all_to_all(array, 'frame', split_axis=0, concat_axis=0, tiled=True)]
    dot_general x5 -> x0, matrix products: 46.3 us -> none  [the longest x1 14.9 us: attend(): jnp.einsum('hqk,khe->qhe', weights, value_heads, preferred_element_type=j...]
    sub x2 -> x0, other arithmetic: 38.7 us -> none  [softmax_rows(): exponent = jnp.exp(scores - row_max)]
    all_to_all x0 -> x1, waiting for transfers between devices: none -> 29.3 us  [regroup(): lax.all_to_all(array, 'frame', split_axis=0, concat_axis=0, tiled=True)]
    pallas_call x0 -> x6, Pallas kernels: none -> 29.1 us  [the longest x3 17.7 us: cond_attention(): pl.pallas_call(functools.partial(cond_kernel, half, width, heads, cuts, l...]
    slice x6 -> x0, local copies, waits for them, and re-layouts: 15.2 us -> none  [the longest x2 5.31 us: attend(): key_heads = keys_values[:, :model_width].reshape(key_count, HEADS, head_dim)]
    convert_element_type x5 -> x0, local copies, waits for them, and re-layouts: 14.9 us -> none  [the longest x3 11.7 us: per_device(): hidden[0, 0].reshape(tokens, model_width).astype(jnp.float32) + mixed_rows]
    reshape x3 -> x1, local copies, waits for them, and re-layouts: 14.4 us -> 0.01 us  [temporal_attention(): norm_gain.reshape(1, width)]
  transfers between devices with their start and end apart: 3 -> 10, of which waited for: 3 -> 4; matrix products, arithmetic and copies ran while one was open for 7% -> 0% of each run, Pallas kernels for 0% -> 9%
where the time goes in v2:
time: 131 us
  waiting for transfers between devices  41.1 us (31%)
  blocking collectives  37.6 us (29%)
  Pallas kernels  29.1 us (22%)
  starting transfers between devices  19.9 us (15%)
  local copies, waits for them, and re-layouts  2.71 us (2%)
    all_to_all x1, blocking collectives, regroup(): lax.all_to_all(array, 'frame', split_axis=0, concat_axis=0, tiled=True)  37.6 us
    all_to_all x1, waiting for transfers between devices, regroup(): lax.all_to_all(array, 'frame', split_axis=0, concat_axis=0, tiled=True)  29.3 us
    pallas_call x3, Pallas kernels, cond_attention(): pl.pallas_call(functools.partial(cond_kernel, half, width, heads, cuts, l...  17.7 us
    pallas_call x1, Pallas kernels, temporal_attention(): pl.pallas_call(temporal_kernel, grid=(3,), in_specs=[whole, pl.BlockSpec(...  11.1 us
    all_to_all x1, starting transfers between devices, regroup(): lax.all_to_all(array, 'frame', split_axis=0, concat_axis=0, tiled=True)  11.1 us
    ppermute x3, waiting for transfers between devices, exchange(): return lax.ppermute(array, axis, [(i, i ^ flip) for i in range(length)])  9.56 us
    ppermute x6, starting transfers between devices, passed_along(): lax.ppermute(array, axis, [(i, (i + by) % length) for i in range(length)])  7.4 us
    unnamed x15, local copies, waits for them, and re-layouts  2.71 us
  transfers between devices with their start and end apart: 10, of which 4 were waited for; matrix products, arithmetic and copies ran while one was open for 0% of the time, Pallas kernels for 9%

profile of v2, /device:TPU:8, one launch (start us, length us, event | category | flops | bytes accessed | tf_op | source)
XLA Modules:
  0.0 130.6 jit_solution(18089106696100007165)
XLA Ops:
  0.0 1.5 %collective-permute-start.1 = (bf16[128,2304]{1,0:T(8,128)(2,1)}, bf16[128,2304]{1,0:T(8,128)(2,1)S(1)}, u32[]{:S(2)}, u32[]{:S(2)}) collective-permute-start(bf16[128,2304]{1,0:T(8,128)(2,1)} %bitcast.20), channel_id=1, source_target_pairs={{0,2},{1,3},{2,0},{3,1},{4,6},{5,7},{6,4},{7,5},{8,10},{9,11},{10,... | collective-permute-start | bytes 1769480 | tf_op jit(solution)/shard_map/ppermute | solution.py:329
  1.5 1.7 %copy-done.2 = bf16[1,1,8,64,2304]{4,3,2,1,0:T(8,128)(2,1)S(1)} copy-done((bf16[1,1,8,64,2304]{4,3,2,1,0:T(8,128)(2,1)S(1)}, bf16[1,1,8,64,2304]{4,3,2,1,0:T(8,128)(2,1)}, u32[]{:S(2)}) %copy-start.2) | copy-done | bytes 2359320
  3.2 0.1 split_halves.3
  3.3 1.7 %collective-permute-start.3 = (bf16[8,32,1024]{2,1,0:T(8,128)(2,1)S(1)}, bf16[8,32,1024]{2,1,0:T(8,128)(2,1)S(1)}, u32[]{:S(2)}, u32[]{:S(2)}) collective-permute-start(bf16[8,32,1024]{2,1,0:T(8,128)(2,1)S(1)} %get-tuple-element.31), channel_id=1, source_target_pairs={{0,64},{64,128},{128,192},{192,0},{1,65},{65,129},{129,193},{193,1... | collective-permute-start | bytes 1572872 | tf_op jit(solution)/shard_map/ppermute | solution.py:334
  5.0 0.0 copy-start.4
  5.0 0.0 copy-start.5
  5.0 0.5 collective-permute-start.4
  5.5 0.2 split_halves.2
  5.7 9.6 %collective-permute-done.1.refs_6_ = bf16[128,2304]{1,0:T(8,128)(2,1)S(1)} collective-permute-done((bf16[128,2304]{1,0:T(8,128)(2,1)}, bf16[128,2304]{1,0:T(8,128)(2,1)S(1)}, u32[]{:S(2)}, u32[]{:S(2)}) %collective-permute-start.1) | collective-permute-done | bytes 589856 | tf_op jit(solution)/shard_map/ppermute | solution.py:329
  15.3 1.6 %collective-permute-start.5 = (bf16[8,32,768]{2,1,0:T(8,128)(2,1)S(1)}, bf16[8,32,768]{2,1,0:T(8,128)(2,1)S(1)}, u32[]{:S(2)}, u32[]{:S(2)}) collective-permute-start(bf16[8,32,768]{2,1,0:T(8,128)(2,1)S(1)} %get-tuple-element.35), channel_id=1, source_target_pairs={{0,64},{64,128},{128,192},{192,0},{1,65},{65,129},{129,193},{193,1... | collective-permute-start | bytes 1179656 | tf_op jit(solution)/shard_map/ppermute | solution.py:334
  16.9 1.6 %collective-permute-start.6 = (bf16[8,32,768]{2,1,0:T(8,128)(2,1)S(1)}, bf16[8,32,768]{2,1,0:T(8,128)(2,1)S(1)}, u32[]{:S(2)}, u32[]{:S(2)}) collective-permute-start(bf16[8,32,768]{2,1,0:T(8,128)(2,1)S(1)} %get-tuple-element.36), channel_id=1, source_target_pairs={{0,192},{64,0},{128,64},{192,128},{1,193},{65,1},{129,65},{193,129... | collective-permute-start | bytes 1179656 | tf_op jit(solution)/shard_map/ppermute | solution.py:334
  18.5 0.9 collective-permute-done.4
  19.4 1.3 collective-permute-start.7
  20.7 0.7 collective-permute-start.8
  21.4 6.1 %cond_attention.3 = (bf16[512,384]{1,0:T(8,128)(2,1)S(1)}, f32[512,128]{1,0:T(8,128)S(1)}) custom-call(s32[1,4]{1,0:T(1,128)S(1)} %copy-done.4, s32[1,2]{1,0:T(1,128)S(1)} %copy-done.5, bf16[512,1152]{1,0:T(8,128)(2,1)S(1)} %bitcast.12, bf16[512,1152]{1,0:T(8,128)(2,1)S(1)} %bitcast.15, bf16[128,2304]{1,0:T(8,128)(2,1)S(1)} %bitcast.22, ...), custom_call_target="tpu_custom_call" | custom-call | tf_op jit(solution)/shard_map/cond_attention/pallas_call | solution.py:184
  27.5 1.3 collective-permute-done.6
  28.8 5.5 %cond_attention.4 = (bf16[512,384]{1,0:T(8,128)(2,1)S(1)}, f32[512,128]{1,0:T(8,128)S(1)}) custom-call(s32[1,4]{1,0:T(1,128)S(1)} %copy-done.4, s32[1,2]{1,0:T(1,128)S(1)} %copy-done.5, bf16[512,1152]{1,0:T(8,128)(2,1)S(1)} %bitcast.13, bf16[512,1152]{1,0:T(8,128)(2,1)S(1)} %bitcast.16, bf16[128,2304]{1,0:T(8,128)(2,1)S(1)} %bitcast.23, ...), custom_call_target="tpu_custom_call" | custom-call | tf_op jit(solution)/shard_map/cond_attention/pallas_call | solution.py:184
  34.4 6.1 %cond_attention.5 = bf16[512,1152]{1,0:T(8,128)(2,1)} custom-call(s32[1,4]{1,0:T(1,128)S(1)} %copy-done.4, s32[1,2]{1,0:T(1,128)S(1)} %copy-done.5, bf16[512,1152]{1,0:T(8,128)(2,1)S(1)} %bitcast.14, bf16[512,1152]{1,0:T(8,128)(2,1)S(1)} %bitcast.17, bf16[128,2304]{1,0:T(8,128)(2,1)S(1)} %bitcast.24, bf16[128,2304]{1,0:T(8,128)(2,1)S(1)} %collective-permute-done.refs_5_, ...), custom_call_target="tpu_custom_call" | custom-call | tf_op jit(solution)/shard_map/cond_attention/pallas_call | solution.py:184
  40.5 0.0 copy-start.6
  40.5 11.1 %all-to-all-start = ((bf16[16,32,1152]{2,1,0:T(8,128)(2,1)}), bf16[16,32,1152]{2,1,0:T(8,128)(2,1)S(1)}, u32[]{:S(2)}, u32[]{:S(2)}) async-start(bf16[16,32,1152]{2,1,0:T(8,128)(2,1)} %bitcast.37), calls=%async_computation | async-start | bytes 2359296 | tf_op jit(solution)/shard_map/all_to_all | solution.py:338
  51.5 29.3 %all-to-all-done.x_ref = bf16[16,32,1152]{2,1,0:T(8,128)(2,1)S(1)} async-done(((bf16[16,32,1152]{2,1,0:T(8,128)(2,1)}), bf16[16,32,1152]{2,1,0:T(8,128)(2,1)S(1)}, u32[]{:S(2)}, u32[]{:S(2)}) %all-to-all-start) | async-done | bytes 1179680 | tf_op jit(solution)/shard_map/all_to_all | solution.py:338
  80.9 11.1 %temporal_attention.1 = bf16[16,32,1152]{2,1,0:T(8,128)(2,1)S(1)} custom-call(bf16[16,32,1152]{2,1,0:T(8,128)(2,1)S(1)} %all-to-all-done.x_ref, f32[1,1152]{1,0:T(1,128)S(1)} %reshape.34.gain_ref, bf16[1152,3456]{1,0:T(8,128)(2,1)} %w_ref.1), custom_call_target="tpu_custom_call" | custom-call | tf_op jit(solution)/shard_map/temporal_attention/pallas_call | solution.py:261
  92.0 37.6 %all_to_all.10 = bf16[16,32,1152]{2,1,0:T(8,128)(2,1)S(1)} all-to-all(bf16[16,32,1152]{2,1,0:T(8,128)(2,1)S(1)} %temporal_attention.1), channel_id=1, replica_groups=mesh['view'=4,'frame'=16,'band'=4] {'frame'}, dimensions={0} | all-to-all | bytes 2359296 | tf_op jit(solution)/shard_map/all_to_all | solution.py:338
  129.6 1.0 copy.10
  (19 shorter events, 0.0 us)
Async XLA Ops:
  0.0 15.3 %collective-permute-start.1 = (bf16[128,2304]{1,0:T(8,128)(2,1)}, bf16[128,2304]{1,0:T(8,128)(2,1)S(1)}, u32[]{:S(2)}, u32[]{:S(2)}) collective-permute-start(bf16[128,2304]{1,0:T(8,128)(2,1)} %bitcast.20), channel_id=1, source_target_pairs={{0,2},{1,3},{2,0},{3,1},{4,6},{5,7},{6,4},{7,5},{8,10},{9,11},{10,... | collective-permute-start | bytes 1769480 | tf_op jit(solution)/shard_map/ppermute | solution.py:329
  1.5 1.7 %copy-start.2 = (bf16[1,1,8,64,2304]{4,3,2,1,0:T(8,128)(2,1)S(1)}, bf16[1,1,8,64,2304]{4,3,2,1,0:T(8,128)(2,1)}, u32[]{:S(2)}) copy-start(bf16[1,1,8,64,2304]{4,3,2,1,0:T(8,128)(2,1)} %param.10) | copy-start | bytes 7077892
  3.2 1.8 %copy-start.3 = (bf16[1,128,2304]{2,1,0:T(8,128)(2,1)S(1)}, bf16[1,128,2304]{2,1,0:T(8,128)(2,1)}, u32[]{:S(2)}) copy-start(bf16[1,128,2304]{2,1,0:T(8,128)(2,1)} %param.11) | copy-start | bytes 1769476
  3.3 13.6 %collective-permute-start.3 = (bf16[8,32,1024]{2,1,0:T(8,128)(2,1)S(1)}, bf16[8,32,1024]{2,1,0:T(8,128)(2,1)S(1)}, u32[]{:S(2)}, u32[]{:S(2)}) collective-permute-start(bf16[8,32,1024]{2,1,0:T(8,128)(2,1)S(1)} %get-tuple-element.31), channel_id=1, source_target_pairs={{0,64},{64,128},{128,192},{192,0},{1,65},{65,129},{129,193},{193,1... | collective-permute-start | bytes 1572872 | tf_op jit(solution)/shard_map/ppermute | solution.py:334
  4.9 15.7 %collective-permute-start = (bf16[128,2304]{1,0:T(8,128)(2,1)S(1)}, bf16[128,2304]{1,0:T(8,128)(2,1)S(1)}, u32[]{:S(2)}, u32[]{:S(2)}) collective-permute-start(bf16[128,2304]{1,0:T(8,128)(2,1)S(1)} %bitcast.21), channel_id=1, source_target_pairs={{0,1},{1,0},{2,3},{3,2},{4,5},{5,4},{6,7},{7,6},{8,9},{9,8},{10,11... | collective-permute-start | bytes 1769480 | tf_op jit(solution)/shard_map/ppermute | solution.py:329
  5.0 16.5 %copy-start = (bf16[1,1,8,64,1152]{4,3,2,1,0:T(8,128)(2,1)S(1)}, bf16[1,1,8,64,1152]{4,3,2,1,0:T(8,128)(2,1)}, u32[]{:S(2)}) copy-start(bf16[1,1,8,64,1152]{4,3,2,1,0:T(8,128)(2,1)} %param.9) | copy-start | bytes 3538948
  5.0 16.5 %copy-start.1 = (bf16[1,1,8,64,1152]{4,3,2,1,0:T(8,128)(2,1)S(1)}, bf16[1,1,8,64,1152]{4,3,2,1,0:T(8,128)(2,1)}, u32[]{:S(2)}) copy-start(bf16[1,1,8,64,1152]{4,3,2,1,0:T(8,128)(2,1)} %param.8) | copy-start | bytes 3538948
  5.0 16.5 %copy-start.4 = (s32[1,4]{1,0:T(1,128)S(1)}, s32[1,4]{1,0:T(1,128)}, u32[]{:S(2)}) copy-start(s32[1,4]{1,0:T(1,128)} %refs_0_.5) | copy-start | bytes 52
  5.0 16.5 %copy-start.5 = (s32[1,2]{1,0:T(1,128)S(1)}, s32[1,2]{1,0:T(1,128)}, u32[]{:S(2)}) copy-start(s32[1,2]{1,0:T(1,128)} %refs_1_.5) | copy-start | bytes 28
  5.0 14.4 %collective-permute-start.4 = (bf16[8,32,1024]{2,1,0:T(8,128)(2,1)S(1)}, bf16[8,32,1024]{2,1,0:T(8,128)(2,1)S(1)}, u32[]{:S(2)}, u32[]{:S(2)}) collective-permute-start(bf16[8,32,1024]{2,1,0:T(8,128)(2,1)S(1)} %get-tuple-element.32), channel_id=1, source_target_pairs={{0,192},{64,0},{128,64},{192,128},{1,193},{65,1},{129,65},{193,129... | collective-permute-start | bytes 1572872 | tf_op jit(solution)/shard_map/ppermute | solution.py:334
  15.3 6.1 %collective-permute-start.2 = (bf16[128,2304]{1,0:T(8,128)(2,1)S(1)}, bf16[128,2304]{1,0:T(8,128)(2,1)S(1)}, u32[]{:S(2)}, u32[]{:S(2)}) collective-permute-start(bf16[128,2304]{1,0:T(8,128)(2,1)S(1)} %collective-permute-done.1.refs_6_), channel_id=1, source_target_pairs={{0,1},{1,0},{2,3},{3,2},{4,5},{5,4},{6,7},{7,6},{8,9},{9,8},{10,11... | collective-permute-start | bytes 1769480 | tf_op jit(solution)/shard_map/ppermute | solution.py:329
  15.3 12.2 %collective-permute-start.5 = (bf16[8,32,768]{2,1,0:T(8,128)(2,1)S(1)}, bf16[8,32,768]{2,1,0:T(8,128)(2,1)S(1)}, u32[]{:S(2)}, u32[]{:S(2)}) collective-permute-start(bf16[8,32,768]{2,1,0:T(8,128)(2,1)S(1)} %get-tuple-element.35), channel_id=1, source_target_pairs={{0,64},{64,128},{128,192},{192,0},{1,65},{65,129},{129,193},{193,1... | collective-permute-start | bytes 1179656 | tf_op jit(solution)/shard_map/ppermute | solution.py:334
  16.9 11.9 %collective-permute-start.6 = (bf16[8,32,768]{2,1,0:T(8,128)(2,1)S(1)}, bf16[8,32,768]{2,1,0:T(8,128)(2,1)S(1)}, u32[]{:S(2)}, u32[]{:S(2)}) collective-permute-start(bf16[8,32,768]{2,1,0:T(8,128)(2,1)S(1)} %get-tuple-element.36), channel_id=1, source_target_pairs={{0,192},{64,0},{128,64},{192,128},{1,193},{65,1},{129,65},{193,129... | collective-permute-start | bytes 1179656 | tf_op jit(solution)/shard_map/ppermute | solution.py:334
  19.4 15.0 %collective-permute-start.7 = (bf16[8,32,512]{2,1,0:T(8,128)(2,1)S(1)}, bf16[8,32,512]{2,1,0:T(8,128)(2,1)S(1)}, u32[]{:S(2)}, u32[]{:S(2)}) collective-permute-start(bf16[8,32,512]{2,1,0:T(8,128)(2,1)S(1)} %get-tuple-element.37), channel_id=1, source_target_pairs={{0,64},{64,128},{128,192},{192,0},{1,65},{65,129},{129,193},{193,1... | collective-permute-start | bytes 786440 | tf_op jit(solution)/shard_map/ppermute | solution.py:334
  20.7 13.7 %collective-permute-start.8 = (bf16[8,32,512]{2,1,0:T(8,128)(2,1)S(1)}, bf16[8,32,512]{2,1,0:T(8,128)(2,1)S(1)}, u32[]{:S(2)}, u32[]{:S(2)}) collective-permute-start(bf16[8,32,512]{2,1,0:T(8,128)(2,1)S(1)} %get-tuple-element.38), channel_id=1, source_target_pairs={{0,192},{64,0},{128,64},{192,128},{1,193},{65,1},{129,65},{193,129... | collective-permute-start | bytes 786440 | tf_op jit(solution)/shard_map/ppermute | solution.py:334
  40.5 11.1 %copy-start.6 = (f32[1152]{0:T(1024)S(1)}, f32[1152]{0:T(1024)}, u32[]{:S(2)}) copy-start(f32[1152]{0:T(1024)} %param.14) | copy-start | bytes 13828
  40.5 40.4 %all-to-all-start = ((bf16[16,32,1152]{2,1,0:T(8,128)(2,1)}), bf16[16,32,1152]{2,1,0:T(8,128)(2,1)S(1)}, u32[]{:S(2)}, u32[]{:S(2)}) async-start(bf16[16,32,1152]{2,1,0:T(8,128)(2,1)} %bitcast.37), calls=%async_computation | async-start | bytes 2359296 | tf_op jit(solution)/shard_map/all_to_all | solution.py:338

commit v3 on v2

--- a/solution.py
+++ b/solution.py
@@ -10,11 +10,13 @@
 
 HEADS = 16
 LANES = 128
-HEAD_STEPS = (0, 6, 11, 16)
-QUERY_ROWS = 256
+HEAD_STEPS = (0, 7, 12, 16)
+QUERY_ROWS = 512
 EPSILON = 1e-06
 DEAD = -1e30
 VMEM_LIMIT = 32 << 20
+LIVE_LAYOUT = 320
+ALIGN = 16
 LOG2E = 1.4426950408889634
 NT = (((1,), (1,)), ((), ()))
 
@@ -54,7 +56,7 @@
     layout_refs = refs[4:8]
     kv_refs = refs[8 : 8 + 2 * count_kv]
     rest = list(refs[8 + 2 * count_kv :])
-    mixed_ref, key_ref, value_ref, sems = rest[-4:]
+    mixed_ref, key_ref, value_ref = rest[-3:]
     last_step = heads[1] == HEADS
     finished = []
     if last_step:
@@ -68,51 +70,56 @@
     keys = kv_refs[0].shape[0]
     slots = layout_refs[0].shape[0]
 
+    band = lax.axis_index("band")
+    limits = [count_ref[0, jnp.bitwise_xor(band, block)] for block in range(len(layout_refs))]
+    offsets = [2 * keys]
+    for limit in limits:
+        offsets.append(offsets[-1] + (limit + ALIGN - 1) // ALIGN * ALIGN)
+
     @pl.when(pl.program_id(0) == 0)
     def _():
-        moves = []
-        for part in range(count_kv):
-            start, end = max(cuts[part], begin), min(cuts[part + 1], finish)
-            size = cuts[part + 1] - cuts[part]
-            for side in range(2 if start < end else 0):
-                low = start - cuts[part]
-                moves.append((kv_refs[2 * part + side], low, size + low, side * keys, start, end))
-        for block, ref in enumerate(layout_refs):
-            at = 2 * keys + block * slots
-            moves.append((ref, begin, width + begin, at, begin, finish))
-        copies = []
-        for which, target in enumerate((key_ref, value_ref)):
-            for move in moves:
-                ref, at, start, end = move[0], move[3], move[4], move[5]
-                low = move[1 + which]
-                copies.append(
-                    pltpu.make_async_copy(
-                        ref.at[:, low : low + end - start],
-                        target.at[at : at + ref.shape[0], start - begin : end - begin],
-                        sems.at[len(copies)],
+        for target, shift in ((key_ref, 0), (value_ref, 1)):
+            for part in range(count_kv):
+                start, end = max(cuts[part], begin), min(cuts[part + 1], finish)
+                size = cuts[part + 1] - cuts[part]
+                low = start - cuts[part] + shift * size
+                for side in range(2 if start < end else 0):
+                    target[side * keys : (side + 1) * keys, start - begin : end - begin] = (
+                        kv_refs[2 * part + side][:, low : low + end - start]
                     )
-                )
-        for copy in copies:
-            copy.start()
-        for copy in copies:
-            copy.wait()
-
-    band = lax.axis_index("band")
+            low = shift * width + begin
+            spare = key_ref.shape[0] - slots
+            columns = slice(low, low + finish - begin)
+            for at in range(2 * keys, spare, slots):
+                target[at : at + slots, :] = layout_refs[0][:, columns]
+            for ref, offset in zip(layout_refs, offsets):
+                at = pl.multiple_of(offset, ALIGN)
+                target[pl.ds(at, slots), :] = ref[:, columns]
+
+    used = key_ref.shape[0] - slots
     column = lax.rem(lane_index(keys), half)
-    live = [column >= half - shared_ref[0, 0], column < shared_ref[0, 1]]
-    for block in range(len(layout_refs)):
-        limit = count_ref[0, jnp.bitwise_xor(band, block)]
-        live.append(lane_index(slots) < limit)
-    bias = jnp.concatenate([jnp.where(mask, 0.0, DEAD) for mask in live], axis=1)
+    slot = lane_index(used - 2 * keys) + 2 * keys
+    layout_live = slot < 0
+    for limit, offset in zip(limits, offsets):
+        layout_live |= (slot >= offset) & (slot < offset + limit)
+    live = jnp.concatenate(
+        [
+            part.astype(jnp.int32)
+            for part in (
+                column >= half - shared_ref[0, 0], column < shared_ref[0, 1], layout_live
+            )
+        ],
+        axis=1,
+    ) > 0
 
     def scores_of(head):
         low, high, first, last = head_span(head, width)
         query = jnp.where(head_mask(head, rows, width), q_ref[:, first:last], jnp.bfloat16(0))
         product = lax.dot_general(
-            query, key_ref[:, first - begin : last - begin], NT,
+            query, key_ref[:used, first - begin : last - begin], NT,
             preferred_element_type=jnp.float32,
         )
-        return product * scale + bias
+        return jnp.where(live, product * scale, DEAD)
 
     done = begin
     if carry_ref is not None:
@@ -125,7 +132,7 @@
         weights = jnp.exp2(scores - over_lanes(jnp.max, jnp.maximum, [scores]))
         total = over_lanes(jnp.sum, jnp.add, [weights])
         mixed = jnp.dot(
-            weights.astype(jnp.bfloat16), value_ref[:, first - begin : last - begin],
+            weights.astype(jnp.bfloat16), value_ref[:used, first - begin : last - begin],
             preferred_element_type=jnp.float32,
         )
         mixed = jnp.where(head_mask(head, rows, width), mixed * (1.0 / total), 0.0)
@@ -166,8 +173,9 @@
     operands = [*scalars, queries, hidden, *layout, *flat]
     specs = [smem, smem, rows_of(read), rows_of(read)]
     specs += [pl.BlockSpec(memory_space=pltpu.VMEM) for _ in (*layout, *flat)]
-    keys = 2 * flat[0].shape[0] + len(layout) * layout[0].shape[0]
-    copies = 2 * (len(layout) + len(flat))
+    slots = layout[0].shape[0]
+    padded = LIVE_LAYOUT + (ALIGN - 1) * len(layout)
+    keys = 2 * flat[0].shape[0] + -(-padded // slots) * slots + slots
     if last_step:
         operands += finished
         specs += [rows_of(array.shape[1]) for array in finished]
@@ -191,7 +199,6 @@
             pltpu.VMEM((QUERY_ROWS, read - begin), jnp.float32),
             pltpu.VMEM((keys, read - begin), jnp.bfloat16),
             pltpu.VMEM((keys, read - begin), jnp.bfloat16),
-            pltpu.SemaphoreType.DMA((copies,)),
         ],
         compiler_params=pltpu.CompilerParams(vmem_limit_bytes=VMEM_LIMIT),
         name="cond_attention",
@@ -228,31 +235,41 @@
     def _():
         row = lax.broadcasted_iota(jnp.int32, (rows, rows), 0)
         column = lax.broadcasted_iota(jnp.int32, (rows, rows), 1)
-        bias = jnp.where(lax.rem(row, group) == lax.rem(column, group), 0.0, DEAD)
-        for at in range(0, positions, group):
+        same = lax.rem(row, group) == lax.rem(column, group)
+
+        def scores_of(at, head):
+            low, high, first, last = head_span(head, width)
             span = slice(at * frames, at * frames + rows)
-            tiles = {}
-            for head in range(HEADS):
-                low, high, first, last = head_span(head, width)
-                mask = head_mask(head, rows, width)
-                query = jnp.where(mask, qkv_ref[span, first:last], jnp.bfloat16(0))
-                key = qkv_ref[span, width + first : width + last]
-                value = qkv_ref[span, 2 * width + first : 2 * width + last]
-                score = lax.dot_general(query, key, NT, preferred_element_type=jnp.float32)
-                score = score * scale + bias
-                weight = jnp.exp2(score - over_lanes(jnp.max, jnp.maximum, [score]))
-                total = over_lanes(jnp.sum, jnp.add, [weight])
-                mixed = jnp.dot(
-                    weight.astype(jnp.bfloat16), value, preferred_element_type=jnp.float32
-                )
-                mixed = jnp.where(mask, mixed * (1.0 / total), 0.0)
-                for tile in range(first, last, LANES):
-                    part = mixed[:, tile - first : tile - first + LANES]
-                    tiles[tile] = tiles[tile] + part if tile in tiles else part
-                    if high >= tile + LANES:
-                        out_ref[:, at : at + group, tile : tile + LANES] = (
-                            tiles.pop(tile).astype(jnp.bfloat16).reshape(frames, group, LANES)
-                        )
+            query = jnp.where(
+                head_mask(head, rows, width), qkv_ref[span, first:last], jnp.bfloat16(0)
+            )
+            key = qkv_ref[span, width + first : width + last]
+            score = lax.dot_general(query, key, NT, preferred_element_type=jnp.float32)
+            return jnp.where(same, score * scale, DEAD)
+
+        turns = [(at, head) for at in range(0, positions, group) for head in range(HEADS)]
+        tiles = {}
+        score = scores_of(*turns[0])
+        for turn, (at, head) in enumerate(turns):
+            following = scores_of(*turns[turn + 1]) if turn + 1 < len(turns) else None
+            low, high, first, last = head_span(head, width)
+            span = slice(at * frames, at * frames + rows)
+            weight = jnp.exp2(score - over_lanes(jnp.max, jnp.maximum, [score]))
+            total = over_lanes(jnp.sum, jnp.add, [weight])
+            mixed = jnp.dot(
+                weight.astype(jnp.bfloat16),
+                qkv_ref[span, 2 * width + first : 2 * width + last],
+                preferred_element_type=jnp.float32,
+            )
+            mixed = jnp.where(head_mask(head, rows, width), mixed * (1.0 / total), 0.0)
+            for tile in range(first, last, LANES):
+                part = mixed[:, tile - first : tile - first + LANES]
+                tiles[tile] = tiles[tile] + part if tile in tiles else part
+                if high >= tile + LANES:
+                    out_ref[:, at : at + group, tile : tile + LANES] = (
+                        tiles.pop(tile).astype(jnp.bfloat16).reshape(frames, group, LANES)
+                    )
+            score = following
 
 
 def temporal_attention(regrouped, norm_gain, w_qkv):
@@ -346,7 +363,7 @@
     tokens = patch_rows * patch_cols
     frames = lax.axis_size("frame")
     cuts = column_cuts(width)
-    own = cond_kv[0, 0]
+    own = pltpu.with_memory_space_constraint(cond_kv[0, 0], pltpu.HBM)
 
     def sent(pair):
         return tuple(

time: 131 us -> 130 us (level)
  local copies, waits for them, and re-layouts: 2.71 us -> 1.05 us
    pallas_call x2, Pallas kernels: 0.33 us -> 2.92 us  [split_halves(): pl.pallas_call(functools.partial(split_kernel, columns // 2, cuts), in_sp...]
    pallas_call x3, Pallas kernels: 17.7 us -> 16 us  [cond_attention(): pl.pallas_call(functools.partial(cond_kernel, half, width, heads, cuts, l...]
    unnamed x15 -> x13, local copies, waits for them, and re-layouts: 2.71 us -> 1.04 us
    all_to_all x1, waiting for transfers between devices: 29.3 us -> 30.7 us  [regroup(): lax.all_to_all(array, 'frame', split_axis=0, concat_axis=0, tiled=True)]
  transfers between devices with their start and end apart: 10 -> 10, of which waited for: 4 -> 6; matrix products, arithmetic and copies ran while one was open for 0% -> 0% of each run, Pallas kernels for 9% -> 11%
where the time goes in v3:
time: 130 us
  waiting for transfers between devices  42.2 us (32%)
  blocking collectives  37.2 us (29%)
  Pallas kernels  29.9 us (23%)
  starting transfers between devices  19.6 us (15%)
    all_to_all x1, blocking collectives, regroup(): lax.all_to_all(array, 'frame', split_axis=0, concat_axis=0, tiled=True)  37.2 us
    all_to_all x1, waiting for transfers between devices, regroup(): lax.all_to_all(array, 'frame', split_axis=0, concat_axis=0, tiled=True)  30.7 us
    pallas_call x3, Pallas kernels, cond_attention(): pl.pallas_call(functools.partial(cond_kernel, half, width, heads, cuts, l...  16 us
    all_to_all x1, starting transfers between devices, regroup(): lax.all_to_all(array, 'frame', split_axis=0, concat_axis=0, tiled=True)  11.2 us
    pallas_call x1, Pallas kernels, temporal_attention(): pl.pallas_call(temporal_kernel, grid=(3,), in_specs=[whole, pl.BlockSpec(...  11 us
    ppermute x3, waiting for transfers between devices, exchange(): return lax.ppermute(array, axis, [(i, i ^ flip) for i in range(length)])  8.63 us
    ppermute x6, starting transfers between devices, passed_along(): lax.ppermute(array, axis, [(i, (i + by) % length) for i in range(length)])  6.9 us
    pallas_call x2, Pallas kernels, split_halves(): pl.pallas_call(functools.partial(split_kernel, columns // 2, cuts), in_sp...  2.92 us
  transfers between devices with their start and end apart: 10, of which 6 were waited for; matrix products, arithmetic and copies ran while one was open for 0% of the time, Pallas kernels for 11%

profile of v3, /device:TPU:8, one launch (start us, length us, event | category | flops | bytes accessed | tf_op | source)
XLA Modules:
  0.0 129.9 jit_solution(14611883904017562168)
XLA Ops:
  0.0 1.5 %collective-permute-start.1 = (bf16[128,2304]{1,0:T(8,128)(2,1)}, bf16[128,2304]{1,0:T(8,128)(2,1)S(1)}, u32[]{:S(2)}, u32[]{:S(2)}) collective-permute-start(bf16[128,2304]{1,0:T(8,128)(2,1)} %bitcast.18), channel_id=1, source_target_pairs={{0,2},{1,3},{2,0},{3,1},{4,6},{5,7},{6,4},{7,5},{8,10},{9,11},{10,... | collective-permute-start | bytes 1769480 | tf_op jit(solution)/shard_map/ppermute | solution.py:346
  1.5 1.3 split_halves.3
  2.8 1.7 %collective-permute-start.3 = (bf16[8,32,1024]{2,1,0:T(8,128)(2,1)S(1)}, bf16[8,32,1024]{2,1,0:T(8,128)(2,1)S(1)}, u32[]{:S(2)}, u32[]{:S(2)}) collective-permute-start(bf16[8,32,1024]{2,1,0:T(8,128)(2,1)S(1)} %get-tuple-element.31), channel_id=1, source_target_pairs={{0,64},{64,128},{128,192},{192,0},{1,65},{65,129},{129,193},{193,1... | collective-permute-start | bytes 1572872 | tf_op jit(solution)/shard_map/ppermute | solution.py:351
  4.5 0.0 copy-start.3
  4.5 0.0 copy-start.4
  4.5 0.5 collective-permute-start.4
  5.0 1.6 %split_halves.2 = (bf16[8,32,768]{2,1,0:T(8,128)(2,1)S(1)}, bf16[8,32,768]{2,1,0:T(8,128)(2,1)S(1)}, bf16[8,32,512]{2,1,0:T(8,128)(2,1)S(1)}, bf16[8,32,512]{2,1,0:T(8,128)(2,1)S(1)}) custom-call(bf16[8,64,2304]{2,1,0:T(8,128)(2,1)} %bitcast.36), custom_call_target="tpu_custom_call" | custom-call | tf_op jit(solution)/shard_map/split_halves/pallas_call | solution.py:332
  6.7 8.6 %collective-permute-done.1.refs_6_ = bf16[128,2304]{1,0:T(8,128)(2,1)S(1)} collective-permute-done((bf16[128,2304]{1,0:T(8,128)(2,1)}, bf16[128,2304]{1,0:T(8,128)(2,1)S(1)}, u32[]{:S(2)}, u32[]{:S(2)}) %collective-permute-start.1) | collective-permute-done | bytes 589856 | tf_op jit(solution)/shard_map/ppermute | solution.py:346
  15.3 1.6 %collective-permute-start.5 = (bf16[8,32,768]{2,1,0:T(8,128)(2,1)S(1)}, bf16[8,32,768]{2,1,0:T(8,128)(2,1)S(1)}, u32[]{:S(2)}, u32[]{:S(2)}) collective-permute-start(bf16[8,32,768]{2,1,0:T(8,128)(2,1)S(1)} %get-tuple-element.35), channel_id=1, source_target_pairs={{0,64},{64,128},{128,192},{192,0},{1,65},{65,129},{129,193},{193,1... | collective-permute-start | bytes 1179656 | tf_op jit(solution)/shard_map/ppermute | solution.py:351
  16.9 1.1 collective-permute-start.6
  18.0 0.9 collective-permute-done.4
  18.9 1.3 collective-permute-start.7
  20.2 0.7 collective-permute-start.8
  20.9 6.0 %cond_attention.3 = (bf16[512,384]{1,0:T(8,128)(2,1)S(1)}, f32[512,128]{1,0:T(8,128)S(1)}) custom-call(s32[1,4]{1,0:T(1,128)S(1)} %copy-done.3, s32[1,2]{1,0:T(1,128)S(1)} %copy-done.4, bf16[512,1152]{1,0:T(8,128)(2,1)S(1)} %bitcast.12, bf16[512,1152]{1,0:T(8,128)(2,1)S(1)} %bitcast.15, bf16[128,2304]{1,0:T(8,128)(2,1)S(1)} %bitcast.20, ...), custom_call_target="tpu_custom_call" | custom-call | tf_op jit(solution)/shard_map/cond_attention/pallas_call | solution.py:192
  27.0 0.2 collective-permute-done.5
  27.2 1.6 %collective-permute-done.6 = bf16[8,32,768]{2,1,0:T(8,128)(2,1)S(1)} collective-permute-done((bf16[8,32,768]{2,1,0:T(8,128)(2,1)S(1)}, bf16[8,32,768]{2,1,0:T(8,128)(2,1)S(1)}, u32[]{:S(2)}, u32[]{:S(2)}) %collective-permute-start.6) | collective-permute-done | bytes 393248 | tf_op jit(solution)/shard_map/ppermute | solution.py:351
  28.8 4.8 %cond_attention.4 = (bf16[512,384]{1,0:T(8,128)(2,1)S(1)}, f32[512,128]{1,0:T(8,128)S(1)}) custom-call(s32[1,4]{1,0:T(1,128)S(1)} %copy-done.3, s32[1,2]{1,0:T(1,128)S(1)} %copy-done.4, bf16[512,1152]{1,0:T(8,128)(2,1)S(1)} %bitcast.13, bf16[512,1152]{1,0:T(8,128)(2,1)S(1)} %bitcast.16, bf16[128,2304]{1,0:T(8,128)(2,1)S(1)} %bitcast.21, ...), custom_call_target="tpu_custom_call" | custom-call | tf_op jit(solution)/shard_map/cond_attention/pallas_call | solution.py:192
  33.6 0.1 collective-permute-done.8
  33.7 5.2 %cond_attention.5 = bf16[512,1152]{1,0:T(8,128)(2,1)} custom-call(s32[1,4]{1,0:T(1,128)S(1)} %copy-done.3, s32[1,2]{1,0:T(1,128)S(1)} %copy-done.4, bf16[512,1152]{1,0:T(8,128)(2,1)S(1)} %bitcast.14, bf16[512,1152]{1,0:T(8,128)(2,1)S(1)} %bitcast.17, bf16[128,2304]{1,0:T(8,128)(2,1)S(1)} %bitcast.22, bf16[128,2304]{1,0:T(8,128)(2,1)S(1)} %collective-permute-done.refs_5_, ...), custom_call_target="tpu_custom_call" | custom-call | tf_op jit(solution)/shard_map/cond_attention/pallas_call | solution.py:192
  38.9 11.2 %all-to-all-start = ((bf16[16,32,1152]{2,1,0:T(8,128)(2,1)}), bf16[16,32,1152]{2,1,0:T(8,128)(2,1)S(1)}, u32[]{:S(2)}, u32[]{:S(2)}) async-start(bf16[16,32,1152]{2,1,0:T(8,128)(2,1)} %bitcast.37), calls=%async_computation | async-start | bytes 2359296 | tf_op jit(solution)/shard_map/all_to_all | solution.py:355
  50.1 30.7 %all-to-all-done.x_ref = bf16[16,32,1152]{2,1,0:T(8,128)(2,1)S(1)} async-done(((bf16[16,32,1152]{2,1,0:T(8,128)(2,1)}), bf16[16,32,1152]{2,1,0:T(8,128)(2,1)S(1)}, u32[]{:S(2)}, u32[]{:S(2)}) %all-to-all-start) | async-done | bytes 1179680 | tf_op jit(solution)/shard_map/all_to_all | solution.py:355
  80.8 11.0 %temporal_attention.1 = bf16[16,32,1152]{2,1,0:T(8,128)(2,1)S(1)} custom-call(bf16[16,32,1152]{2,1,0:T(8,128)(2,1)S(1)} %all-to-all-done.x_ref, f32[1,1152]{1,0:T(1,128)S(1)} %reshape.34.gain_ref, bf16[1152,3456]{1,0:T(8,128)(2,1)} %w_ref.1), custom_call_target="tpu_custom_call" | custom-call | tf_op jit(solution)/shard_map/temporal_attention/pallas_call | solution.py:278
  91.8 37.2 %all_to_all.10 = bf16[16,32,1152]{2,1,0:T(8,128)(2,1)S(1)} all-to-all(bf16[16,32,1152]{2,1,0:T(8,128)(2,1)S(1)} %temporal_attention.1), channel_id=1, replica_groups=mesh['view'=4,'frame'=16,'band'=4] {'frame'}, dimensions={0} | all-to-all | bytes 2359296 | tf_op jit(solution)/shard_map/all_to_all | solution.py:355
  128.9 1.0 copy.10
  (17 shorter events, 0.0 us)
Async XLA Ops:
  0.0 15.3 %collective-permute-start.1 = (bf16[128,2304]{1,0:T(8,128)(2,1)}, bf16[128,2304]{1,0:T(8,128)(2,1)S(1)}, u32[]{:S(2)}, u32[]{:S(2)}) collective-permute-start(bf16[128,2304]{1,0:T(8,128)(2,1)} %bitcast.18), channel_id=1, source_target_pairs={{0,2},{1,3},{2,0},{3,1},{4,6},{5,7},{6,4},{7,5},{8,10},{9,11},{10,... | collective-permute-start | bytes 1769480 | tf_op jit(solution)/shard_map/ppermute | solution.py:346
  1.5 3.0 %copy-start.2 = (bf16[1,128,2304]{2,1,0:T(8,128)(2,1)S(1)}, bf16[1,128,2304]{2,1,0:T(8,128)(2,1)}, u32[]{:S(2)}) copy-start(bf16[1,128,2304]{2,1,0:T(8,128)(2,1)} %param.11) | copy-start | bytes 1769476
  2.8 14.1 %collective-permute-start.3 = (bf16[8,32,1024]{2,1,0:T(8,128)(2,1)S(1)}, bf16[8,32,1024]{2,1,0:T(8,128)(2,1)S(1)}, u32[]{:S(2)}, u32[]{:S(2)}) collective-permute-start(bf16[8,32,1024]{2,1,0:T(8,128)(2,1)S(1)} %get-tuple-element.31), channel_id=1, source_target_pairs={{0,64},{64,128},{128,192},{192,0},{1,65},{65,129},{129,193},{193,1... | collective-permute-start | bytes 1572872 | tf_op jit(solution)/shard_map/ppermute | solution.py:351
  4.5 15.7 %collective-permute-start = (bf16[128,2304]{1,0:T(8,128)(2,1)S(1)}, bf16[128,2304]{1,0:T(8,128)(2,1)S(1)}, u32[]{:S(2)}, u32[]{:S(2)}) collective-permute-start(bf16[128,2304]{1,0:T(8,128)(2,1)S(1)} %bitcast.19), channel_id=1, source_target_pairs={{0,1},{1,0},{2,3},{3,2},{4,5},{5,4},{6,7},{7,6},{8,9},{9,8},{10,11... | collective-permute-start | bytes 1769480 | tf_op jit(solution)/shard_map/ppermute | solution.py:346
  4.5 16.5 %copy-start = (bf16[1,1,8,64,1152]{4,3,2,1,0:T(8,128)(2,1)S(1)}, bf16[1,1,8,64,1152]{4,3,2,1,0:T(8,128)(2,1)}, u32[]{:S(2)}) copy-start(bf16[1,1,8,64,1152]{4,3,2,1,0:T(8,128)(2,1)} %param.9) | copy-start | bytes 3538948
  4.5 16.5 %copy-start.1 = (bf16[1,1,8,64,1152]{4,3,2,1,0:T(8,128)(2,1)S(1)}, bf16[1,1,8,64,1152]{4,3,2,1,0:T(8,128)(2,1)}, u32[]{:S(2)}) copy-start(bf16[1,1,8,64,1152]{4,3,2,1,0:T(8,128)(2,1)} %param.8) | copy-start | bytes 3538948
  4.5 16.5 %copy-start.3 = (s32[1,4]{1,0:T(1,128)S(1)}, s32[1,4]{1,0:T(1,128)}, u32[]{:S(2)}) copy-start(s32[1,4]{1,0:T(1,128)} %refs_0_.5) | copy-start | bytes 52
  4.5 16.5 %copy-start.4 = (s32[1,2]{1,0:T(1,128)S(1)}, s32[1,2]{1,0:T(1,128)}, u32[]{:S(2)}) copy-start(s32[1,2]{1,0:T(1,128)} %refs_1_.5) | copy-start | bytes 28
  4.5 14.4 %collective-permute-start.4 = (bf16[8,32,1024]{2,1,0:T(8,128)(2,1)S(1)}, bf16[8,32,1024]{2,1,0:T(8,128)(2,1)S(1)}, u32[]{:S(2)}, u32[]{:S(2)}) collective-permute-start(bf16[8,32,1024]{2,1,0:T(8,128)(2,1)S(1)} %get-tuple-element.32), channel_id=1, source_target_pairs={{0,192},{64,0},{128,64},{192,128},{1,193},{65,1},{129,65},{193,129... | collective-permute-start | bytes 1572872 | tf_op jit(solution)/shard_map/ppermute | solution.py:351
  15.3 5.6 %collective-permute-start.2 = (bf16[128,2304]{1,0:T(8,128)(2,1)S(1)}, bf16[128,2304]{1,0:T(8,128)(2,1)S(1)}, u32[]{:S(2)}, u32[]{:S(2)}) collective-permute-start(bf16[128,2304]{1,0:T(8,128)(2,1)S(1)} %collective-permute-done.1.refs_6_), channel_id=1, source_target_pairs={{0,1},{1,0},{2,3},{3,2},{4,5},{5,4},{6,7},{7,6},{8,9},{9,8},{10,11... | collective-permute-start | bytes 1769480 | tf_op jit(solution)/shard_map/ppermute | solution.py:346
  15.3 11.9 %collective-permute-start.5 = (bf16[8,32,768]{2,1,0:T(8,128)(2,1)S(1)}, bf16[8,32,768]{2,1,0:T(8,128)(2,1)S(1)}, u32[]{:S(2)}, u32[]{:S(2)}) collective-permute-start(bf16[8,32,768]{2,1,0:T(8,128)(2,1)S(1)} %get-tuple-element.35), channel_id=1, source_target_pairs={{0,64},{64,128},{128,192},{192,0},{1,65},{65,129},{129,193},{193,1... | collective-permute-start | bytes 1179656 | tf_op jit(solution)/shard_map/ppermute | solution.py:351
  16.9 11.9 %collective-permute-start.6 = (bf16[8,32,768]{2,1,0:T(8,128)(2,1)S(1)}, bf16[8,32,768]{2,1,0:T(8,128)(2,1)S(1)}, u32[]{:S(2)}, u32[]{:S(2)}) collective-permute-start(bf16[8,32,768]{2,1,0:T(8,128)(2,1)S(1)} %get-tuple-element.36), channel_id=1, source_target_pairs={{0,192},{64,0},{128,64},{192,128},{1,193},{65,1},{129,65},{193,129... | collective-permute-start | bytes 1179656 | tf_op jit(solution)/shard_map/ppermute | solution.py:351
  18.9 14.7 %collective-permute-start.7 = (bf16[8,32,512]{2,1,0:T(8,128)(2,1)S(1)}, bf16[8,32,512]{2,1,0:T(8,128)(2,1)S(1)}, u32[]{:S(2)}, u32[]{:S(2)}) collective-permute-start(bf16[8,32,512]{2,1,0:T(8,128)(2,1)S(1)} %get-tuple-element.37), channel_id=1, source_target_pairs={{0,64},{64,128},{128,192},{192,0},{1,65},{65,129},{129,193},{193,1... | collective-permute-start | bytes 786440 | tf_op jit(solution)/shard_map/ppermute | solution.py:351
  20.2 13.6 %collective-permute-start.8 = (bf16[8,32,512]{2,1,0:T(8,128)(2,1)S(1)}, bf16[8,32,512]{2,1,0:T(8,128)(2,1)S(1)}, u32[]{:S(2)}, u32[]{:S(2)}) collective-permute-start(bf16[8,32,512]{2,1,0:T(8,128)(2,1)S(1)} %get-tuple-element.38), channel_id=1, source_target_pairs={{0,192},{64,0},{128,64},{192,128},{1,193},{65,1},{129,65},{193,129... | collective-permute-start | bytes 786440 | tf_op jit(solution)/shard_map/ppermute | solution.py:351
  38.9 11.2 %copy-start.5 = (f32[1152]{0:T(1024)S(1)}, f32[1152]{0:T(1024)}, u32[]{:S(2)}) copy-start(f32[1152]{0:T(1024)} %param.14) | copy-start | bytes 13828
  38.9 41.9 %all-to-all-start = ((bf16[16,32,1152]{2,1,0:T(8,128)(2,1)}), bf16[16,32,1152]{2,1,0:T(8,128)(2,1)S(1)}, u32[]{:S(2)}, u32[]{:S(2)}) async-start(bf16[16,32,1152]{2,1,0:T(8,128)(2,1)} %bitcast.37), calls=%async_computation | async-start | bytes 2359296 | tf_op jit(solution)/shard_map/all_to_all | solution.py:355

commit v4 on v3

--- a/solution.py
+++ b/solution.py
@@ -10,8 +10,7 @@
 
 HEADS = 16
 LANES = 128
-HEAD_STEPS = (0, 7, 12, 16)
-QUERY_ROWS = 512
+HEAD_STEPS = (0, 8, 12, 16)
 EPSILON = 1e-06
 DEAD = -1e30
 VMEM_LIMIT = 32 << 20
@@ -56,7 +55,7 @@
     layout_refs = refs[4:8]
     kv_refs = refs[8 : 8 + 2 * count_kv]
     rest = list(refs[8 + 2 * count_kv :])
-    mixed_ref, key_ref, value_ref = rest[-3:]
+    mixed_ref, key_ref, value_ref, state_ref, sems = rest[-5:]
     last_step = heads[1] == HEADS
     finished = []
     if last_step:
@@ -70,31 +69,39 @@
     keys = kv_refs[0].shape[0]
     slots = layout_refs[0].shape[0]
 
+    moves = []
+    if last_step:
+        at = 0
+        for index, ref in enumerate((*finished, state_ref)):
+            columns = slice(at, at + ref.shape[1])
+            moves.append(pltpu.make_async_copy(ref, out_ref.at[:, columns], sems.at[index]))
+            at += ref.shape[1]
+        for move in moves[:-1]:
+            move.start()
+
     band = lax.axis_index("band")
     limits = [count_ref[0, jnp.bitwise_xor(band, block)] for block in range(len(layout_refs))]
     offsets = [2 * keys]
     for limit in limits:
         offsets.append(offsets[-1] + (limit + ALIGN - 1) // ALIGN * ALIGN)
 
-    @pl.when(pl.program_id(0) == 0)
-    def _():
-        for target, shift in ((key_ref, 0), (value_ref, 1)):
-            for part in range(count_kv):
-                start, end = max(cuts[part], begin), min(cuts[part + 1], finish)
-                size = cuts[part + 1] - cuts[part]
-                low = start - cuts[part] + shift * size
-                for side in range(2 if start < end else 0):
-                    target[side * keys : (side + 1) * keys, start - begin : end - begin] = (
-                        kv_refs[2 * part + side][:, low : low + end - start]
-                    )
-            low = shift * width + begin
-            spare = key_ref.shape[0] - slots
-            columns = slice(low, low + finish - begin)
-            for at in range(2 * keys, spare, slots):
-                target[at : at + slots, :] = layout_refs[0][:, columns]
-            for ref, offset in zip(layout_refs, offsets):
-                at = pl.multiple_of(offset, ALIGN)
-                target[pl.ds(at, slots), :] = ref[:, columns]
+    for target, shift in ((key_ref, 0), (value_ref, 1)):
+        for part in range(count_kv):
+            start, end = max(cuts[part], begin), min(cuts[part + 1], finish)
+            size = cuts[part + 1] - cuts[part]
+            low = start - cuts[part] + shift * size
+            for side in range(2 if start < end else 0):
+                target[side * keys : (side + 1) * keys, start - begin : end - begin] = (
+                    kv_refs[2 * part + side][:, low : low + end - start]
+                )
+        low = shift * width + begin
+        spare = key_ref.shape[0] - slots
+        columns = slice(low, low + finish - begin)
+        for at in range(2 * keys, spare, slots):
+            target[at : at + slots, :] = layout_refs[0][:, columns]
+        for ref, offset in zip(layout_refs, offsets):
+            at = pl.multiple_of(offset, ALIGN)
+            target[pl.ds(at, slots), :] = ref[:, columns]
 
     used = key_ref.shape[0] - slots
     column = lax.rem(lane_index(keys), half)
@@ -144,14 +151,17 @@
                 mixed_ref[:, at - begin : at - begin + LANES] = part
                 done = at + LANES
         scores = following
-    at = 0
-    for ref in finished:
-        out_ref[:, at : at + ref.shape[1]] = ref[...]
-        at += ref.shape[1]
-    size = out_ref.shape[1] - at
-    out_ref[:, at:] = (
+    size = finish - begin if last_step else out_ref.shape[1]
+    state = (
         hidden_ref[:, begin : begin + size].astype(jnp.float32) + mixed_ref[:, :size]
     ).astype(jnp.bfloat16)
+    if last_step:
+        state_ref[...] = state
+        moves[-1].start()
+        for move in moves:
+            move.wait()
+    else:
+        out_ref[...] = state
     if not last_step:
         rest[1][...] = mixed_ref[:, size : size + LANES]
 
@@ -167,7 +177,7 @@
     smem = pl.BlockSpec(memory_space=pltpu.SMEM)
 
     def rows_of(columns):
-        return pl.BlockSpec((QUERY_ROWS, columns), lambda i: (i, 0))
+        return pl.BlockSpec((tokens, columns), lambda i: (i, 0))
 
     flat = [array for pair in kv_parts for array in pair]
     operands = [*scalars, queries, hidden, *layout, *flat]
@@ -182,7 +192,7 @@
     if carry is not None:
         operands.append(carry)
         specs.append(rows_of(LANES))
-    out_specs = [rows_of(size)]
+    out_specs = [pl.BlockSpec(memory_space=pltpu.HBM) if last_step else rows_of(size)]
     out_shape = [jax.ShapeDtypeStruct((tokens, size), jnp.bfloat16)]
     if last_step:
         out_shape = [pltpu.HBM((tokens, size), jnp.bfloat16)]
@@ -191,14 +201,16 @@
         out_shape.append(jax.ShapeDtypeStruct((tokens, LANES), jnp.float32))
     return pl.pallas_call(
         functools.partial(cond_kernel, half, width, heads, cuts, len(kv_parts)),
-        grid=(tokens // QUERY_ROWS,),
+        grid=(1,),
         in_specs=specs,
         out_specs=out_specs,
         out_shape=out_shape,
         scratch_shapes=[
-            pltpu.VMEM((QUERY_ROWS, read - begin), jnp.float32),
+            pltpu.VMEM((tokens, read - begin), jnp.float32),
             pltpu.VMEM((keys, read - begin), jnp.bfloat16),
             pltpu.VMEM((keys, read - begin), jnp.bfloat16),
+            pltpu.VMEM((tokens, width - begin if last_step else LANES), jnp.bfloat16),
+            pltpu.SemaphoreType.DMA((len(HEAD_STEPS) - 1,)),
         ],
         compiler_params=pltpu.CompilerParams(vmem_limit_bytes=VMEM_LIMIT),
         name="cond_attention",

time: 130 us -> 128 us (0.985); the launches traced: 130 us -> 126 us
  blocking collectives: 37.2 us -> 34.6 us
    all_to_all x1, blocking collectives: 37.2 us -> 34.6 us  [regroup(): lax.all_to_all(array, 'frame', split_axis=0, concat_axis=0, tiled=True)]
  transfers between devices with their start and end apart: 10 -> 10, of which waited for: 6 -> 3; matrix products, arithmetic and copies ran while one was open for 0% -> 0% of each run, Pallas kernels for 11% -> 11%
where the time goes in v4:
time: 128 us; the launch traced here: 126 us
  waiting for transfers between devices  41.1 us (32%)
  blocking collectives  34.6 us (27%)
  Pallas kernels  29.6 us (23%)
  starting transfers between devices  19.5 us (15%)
    all_to_all x1, blocking collectives, regroup(): lax.all_to_all(array, 'frame', split_axis=0, concat_axis=0, tiled=True)  34.6 us
    all_to_all x1, waiting for transfers between devices, regroup(): lax.all_to_all(array, 'frame', split_axis=0, concat_axis=0, tiled=True)  29.5 us
    pallas_call x3, Pallas kernels, cond_attention(): pl.pallas_call(functools.partial(cond_kernel, half, width, heads, cuts, l...  15.7 us
    pallas_call x1, Pallas kernels, temporal_attention(): pl.pallas_call(temporal_kernel, grid=(3,), in_specs=[whole, pl.BlockSpec(...  11 us
    all_to_all x1, starting transfers between devices, regroup(): lax.all_to_all(array, 'frame', split_axis=0, concat_axis=0, tiled=True)  10.5 us
    ppermute x3, waiting for transfers between devices, exchange(): return lax.ppermute(array, axis, [(i, i ^ flip) for i in range(length)])  8.64 us
    ppermute x6, starting transfers between devices, passed_along(): lax.ppermute(array, axis, [(i, (i + by) % length) for i in range(length)])  7.51 us
    ppermute x6, waiting for transfers between devices, passed_along(): lax.ppermute(array, axis, [(i, (i + by) % length) for i in range(length)])  3 us
  transfers between devices with their start and end apart: 10, of which 3 were waited for; matrix products, arithmetic and copies ran while one was open for 0% of the time, Pallas kernels for 11%

profile of v4, /device:TPU:8, one launch (start us, length us, event | category | flops | bytes accessed | tf_op | source)
XLA Modules:
  0.0 126.0 jit_solution(3026343694058157005)
XLA Ops:
  0.0 1.5 %collective-permute-start.1 = (bf16[128,2304]{1,0:T(8,128)(2,1)}, bf16[128,2304]{1,0:T(8,128)(2,1)S(1)}, u32[]{:S(2)}, u32[]{:S(2)}) collective-permute-start(bf16[128,2304]{1,0:T(8,128)(2,1)} %bitcast.24), channel_id=1, source_target_pairs={{0,2},{1,3},{2,0},{3,1},{4,6},{5,7},{6,4},{7,5},{8,10},{9,11},{10,... | collective-permute-start | bytes 1769480 | tf_op jit(solution)/shard_map/ppermute | solution.py:358
  1.5 1.4 %split_halves.3 = (bf16[8,32,1280]{2,1,0:T(8,128)(2,1)S(1)}, bf16[8,32,1280]{2,1,0:T(8,128)(2,1)S(1)}) custom-call(bf16[8,64,2304]{2,1,0:T(8,128)(2,1)} %bitcast.35), custom_call_target="tpu_custom_call" | custom-call | tf_op jit(solution)/shard_map/split_halves/pallas_call | solution.py:344
  2.9 1.7 %collective-permute-start.3 = (bf16[8,32,1280]{2,1,0:T(8,128)(2,1)S(1)}, bf16[8,32,1280]{2,1,0:T(8,128)(2,1)S(1)}, u32[]{:S(2)}, u32[]{:S(2)}) collective-permute-start(bf16[8,32,1280]{2,1,0:T(8,128)(2,1)S(1)} %get-tuple-element.31), channel_id=1, source_target_pairs={{0,64},{64,128},{128,192},{192,0},{1,65},{65,129},{129,193},{193,1... | collective-permute-start | bytes 1966088 | tf_op jit(solution)/shard_map/ppermute | solution.py:363
  4.5 0.5 collective-permute-start.4
  5.1 1.6 %split_halves.2 = (bf16[8,32,512]{2,1,0:T(8,128)(2,1)S(1)}, bf16[8,32,512]{2,1,0:T(8,128)(2,1)S(1)}, bf16[8,32,512]{2,1,0:T(8,128)(2,1)S(1)}, bf16[8,32,512]{2,1,0:T(8,128)(2,1)S(1)}) custom-call(bf16[8,64,2304]{2,1,0:T(8,128)(2,1)} %bitcast.36), custom_call_target="tpu_custom_call" | custom-call | tf_op jit(solution)/shard_map/split_halves/pallas_call | solution.py:344
  6.6 8.6 %collective-permute-done.1.refs_6_ = bf16[128,2304]{1,0:T(8,128)(2,1)S(1)} collective-permute-done((bf16[128,2304]{1,0:T(8,128)(2,1)}, bf16[128,2304]{1,0:T(8,128)(2,1)S(1)}, u32[]{:S(2)}, u32[]{:S(2)}) %collective-permute-start.1) | collective-permute-done | bytes 589856 | tf_op jit(solution)/shard_map/ppermute | solution.py:358
  15.3 1.6 %collective-permute-start.5 = (bf16[8,32,512]{2,1,0:T(8,128)(2,1)S(1)}, bf16[8,32,512]{2,1,0:T(8,128)(2,1)S(1)}, u32[]{:S(2)}, u32[]{:S(2)}) collective-permute-start(bf16[8,32,512]{2,1,0:T(8,128)(2,1)S(1)} %get-tuple-element.35), channel_id=1, source_target_pairs={{0,64},{64,128},{128,192},{192,0},{1,65},{65,129},{129,193},{193,1... | collective-permute-start | bytes 786440 | tf_op jit(solution)/shard_map/ppermute | solution.py:363
  16.9 3.0 %collective-permute-done.3 = bf16[8,32,1280]{2,1,0:T(8,128)(2,1)S(1)} collective-permute-done((bf16[8,32,1280]{2,1,0:T(8,128)(2,1)S(1)}, bf16[8,32,1280]{2,1,0:T(8,128)(2,1)S(1)}, u32[]{:S(2)}, u32[]{:S(2)}) %collective-permute-start.3) | collective-permute-done | bytes 655392 | tf_op jit(solution)/shard_map/ppermute | solution.py:363
  19.8 1.7 %collective-permute-start.6 = (bf16[8,32,512]{2,1,0:T(8,128)(2,1)S(1)}, bf16[8,32,512]{2,1,0:T(8,128)(2,1)S(1)}, u32[]{:S(2)}, u32[]{:S(2)}) collective-permute-start(bf16[8,32,512]{2,1,0:T(8,128)(2,1)S(1)} %get-tuple-element.36), channel_id=1, source_target_pairs={{0,192},{64,0},{128,64},{192,128},{1,193},{65,1},{129,65},{193,129... | collective-permute-start | bytes 786440 | tf_op jit(solution)/shard_map/ppermute | solution.py:363
  21.6 0.0 collective-permute-done.4
  21.6 0.3 collective-permute-start.7
  21.9 0.0 collective-permute-done.refs_5_
  21.9 1.7 %collective-permute-start.8 = (bf16[8,32,512]{2,1,0:T(8,128)(2,1)S(1)}, bf16[8,32,512]{2,1,0:T(8,128)(2,1)S(1)}, u32[]{:S(2)}, u32[]{:S(2)}) collective-permute-start(bf16[8,32,512]{2,1,0:T(8,128)(2,1)S(1)} %get-tuple-element.38), channel_id=1, source_target_pairs={{0,192},{64,0},{128,64},{192,128},{1,193},{65,1},{129,65},{193,129... | collective-permute-start | bytes 786440 | tf_op jit(solution)/shard_map/ppermute | solution.py:363
  23.6 0.0 collective-permute-done.2.refs_7_
  23.6 7.0 %cond_attention.3 = (bf16[512,512]{1,0:T(8,128)(2,1)S(1)}, f32[512,128]{1,0:T(8,128)S(1)}) custom-call(s32[1,4]{1,0:T(1,128)S(1)} %copy-done.3, s32[1,2]{1,0:T(1,128)S(1)} %copy-done.4, bf16[512,1152]{1,0:T(8,128)(2,1)S(1)} %bitcast.12, bf16[512,1152]{1,0:T(8,128)(2,1)S(1)} %bitcast.15, bf16[128,2304]{1,0:T(8,128)(2,1)S(1)} %bitcast.26, ...), custom_call_target="tpu_custom_call" | custom-call | tf_op jit(solution)/shard_map/cond_attention/pallas_call | solution.py:202
  30.6 0.0 collective-permute-done.5
  30.6 3.8 %cond_attention.4 = (bf16[512,256]{1,0:T(8,128)(2,1)S(1)}, f32[512,128]{1,0:T(8,128)S(1)}) custom-call(s32[1,4]{1,0:T(1,128)S(1)} %copy-done.3, s32[1,2]{1,0:T(1,128)S(1)} %copy-done.4, bf16[512,1152]{1,0:T(8,128)(2,1)S(1)} %bitcast.13, bf16[512,1152]{1,0:T(8,128)(2,1)S(1)} %bitcast.16, bf16[128,2304]{1,0:T(8,128)(2,1)S(1)} %bitcast.27, ...), custom_call_target="tpu_custom_call" | custom-call | tf_op jit(solution)/shard_map/cond_attention/pallas_call | solution.py:202
  34.5 4.9 %cond_attention.5 = bf16[512,1152]{1,0:T(8,128)(2,1)} custom-call(s32[1,4]{1,0:T(1,128)S(1)} %copy-done.3, s32[1,2]{1,0:T(1,128)S(1)} %copy-done.4, bf16[512,1152]{1,0:T(8,128)(2,1)S(1)} %bitcast.14, bf16[512,1152]{1,0:T(8,128)(2,1)S(1)} %bitcast.17, bf16[128,2304]{1,0:T(8,128)(2,1)S(1)} %bitcast.28, bf16[128,2304]{1,0:T(8,128)(2,1)S(1)} %collective-permute-done.refs_5_, ...), custom_call_target="tpu_custom_call" | custom-call | tf_op jit(solution)/shard_map/cond_attention/pallas_call | solution.py:202
  39.4 0.0 copy-start.5
  39.4 10.5 %all-to-all-start = ((bf16[16,32,1152]{2,1,0:T(8,128)(2,1)}), bf16[16,32,1152]{2,1,0:T(8,128)(2,1)S(1)}, u32[]{:S(2)}, u32[]{:S(2)}) async-start(bf16[16,32,1152]{2,1,0:T(8,128)(2,1)} %bitcast.37), calls=%async_computation | async-start | bytes 2359296 | tf_op jit(solution)/shard_map/all_to_all | solution.py:367
  49.9 29.5 %all-to-all-done.x_ref = bf16[16,32,1152]{2,1,0:T(8,128)(2,1)S(1)} async-done(((bf16[16,32,1152]{2,1,0:T(8,128)(2,1)}), bf16[16,32,1152]{2,1,0:T(8,128)(2,1)S(1)}, u32[]{:S(2)}, u32[]{:S(2)}) %all-to-all-start) | async-done | bytes 1179680 | tf_op jit(solution)/shard_map/all_to_all | solution.py:367
  79.4 11.0 %temporal_attention.1 = bf16[16,32,1152]{2,1,0:T(8,128)(2,1)S(1)} custom-call(bf16[16,32,1152]{2,1,0:T(8,128)(2,1)S(1)} %all-to-all-done.x_ref, f32[1,1152]{1,0:T(1,128)S(1)} %reshape.34.gain_ref, bf16[1152,3456]{1,0:T(8,128)(2,1)} %w_ref.1), custom_call_target="tpu_custom_call" | custom-call | tf_op jit(solution)/shard_map/temporal_attention/pallas_call | solution.py:290
  90.4 34.6 %all_to_all.10 = bf16[16,32,1152]{2,1,0:T(8,128)(2,1)S(1)} all-to-all(bf16[16,32,1152]{2,1,0:T(8,128)(2,1)S(1)} %temporal_attention.1), channel_id=1, replica_groups=mesh['view'=4,'frame'=16,'band'=4] {'frame'}, dimensions={0} | all-to-all | bytes 2359296 | tf_op jit(solution)/shard_map/all_to_all | solution.py:367
  125.0 1.0 copy.10
  (17 shorter events, 0.0 us)
Async XLA Ops:
  0.0 15.3 %collective-permute-start.1 = (bf16[128,2304]{1,0:T(8,128)(2,1)}, bf16[128,2304]{1,0:T(8,128)(2,1)S(1)}, u32[]{:S(2)}, u32[]{:S(2)}) collective-permute-start(bf16[128,2304]{1,0:T(8,128)(2,1)} %bitcast.24), channel_id=1, source_target_pairs={{0,2},{1,3},{2,0},{3,1},{4,6},{5,7},{6,4},{7,5},{8,10},{9,11},{10,... | collective-permute-start | bytes 1769480 | tf_op jit(solution)/shard_map/ppermute | solution.py:358
  1.5 3.6 %copy-start.2 = (bf16[1,128,2304]{2,1,0:T(8,128)(2,1)S(1)}, bf16[1,128,2304]{2,1,0:T(8,128)(2,1)}, u32[]{:S(2)}) copy-start(bf16[1,128,2304]{2,1,0:T(8,128)(2,1)} %param.11) | copy-start | bytes 1769476
  2.9 17.0 %collective-permute-start.3 = (bf16[8,32,1280]{2,1,0:T(8,128)(2,1)S(1)}, bf16[8,32,1280]{2,1,0:T(8,128)(2,1)S(1)}, u32[]{:S(2)}, u32[]{:S(2)}) collective-permute-start(bf16[8,32,1280]{2,1,0:T(8,128)(2,1)S(1)} %get-tuple-element.31), channel_id=1, source_target_pairs={{0,64},{64,128},{128,192},{192,0},{1,65},{65,129},{129,193},{193,1... | collective-permute-start | bytes 1966088 | tf_op jit(solution)/shard_map/ppermute | solution.py:363
  4.5 19.1 %copy-start = (bf16[1,1,8,64,1152]{4,3,2,1,0:T(8,128)(2,1)S(1)}, bf16[1,1,8,64,1152]{4,3,2,1,0:T(8,128)(2,1)}, u32[]{:S(2)}) copy-start(bf16[1,1,8,64,1152]{4,3,2,1,0:T(8,128)(2,1)} %param.9) | copy-start | bytes 3538948
  4.5 19.1 %copy-start.1 = (bf16[1,1,8,64,1152]{4,3,2,1,0:T(8,128)(2,1)S(1)}, bf16[1,1,8,64,1152]{4,3,2,1,0:T(8,128)(2,1)}, u32[]{:S(2)}) copy-start(bf16[1,1,8,64,1152]{4,3,2,1,0:T(8,128)(2,1)} %param.8) | copy-start | bytes 3538948
  4.5 19.1 %copy-start.3 = (s32[1,4]{1,0:T(1,128)S(1)}, s32[1,4]{1,0:T(1,128)}, u32[]{:S(2)}) copy-start(s32[1,4]{1,0:T(1,128)} %refs_0_.5) | copy-start | bytes 52
  4.5 19.1 %copy-start.4 = (s32[1,2]{1,0:T(1,128)S(1)}, s32[1,2]{1,0:T(1,128)}, u32[]{:S(2)}) copy-start(s32[1,2]{1,0:T(1,128)} %refs_1_.5) | copy-start | bytes 28
  4.5 17.0 %collective-permute-start.4 = (bf16[8,32,1280]{2,1,0:T(8,128)(2,1)S(1)}, bf16[8,32,1280]{2,1,0:T(8,128)(2,1)S(1)}, u32[]{:S(2)}, u32[]{:S(2)}) collective-permute-start(bf16[8,32,1280]{2,1,0:T(8,128)(2,1)S(1)} %get-tuple-element.32), channel_id=1, source_target_pairs={{0,192},{64,0},{128,64},{192,128},{1,193},{65,1},{129,65},{193,129... | collective-permute-start | bytes 1966088 | tf_op jit(solution)/shard_map/ppermute | solution.py:363
  5.1 16.8 %collective-permute-start = (bf16[128,2304]{1,0:T(8,128)(2,1)S(1)}, bf16[128,2304]{1,0:T(8,128)(2,1)S(1)}, u32[]{:S(2)}, u32[]{:S(2)}) collective-permute-start(bf16[128,2304]{1,0:T(8,128)(2,1)S(1)} %bitcast.25), channel_id=1, source_target_pairs={{0,1},{1,0},{2,3},{3,2},{4,5},{5,4},{6,7},{7,6},{8,9},{9,8},{10,11... | collective-permute-start | bytes 1769480 | tf_op jit(solution)/shard_map/ppermute | solution.py:358
  15.3 8.3 %collective-permute-start.2 = (bf16[128,2304]{1,0:T(8,128)(2,1)S(1)}, bf16[128,2304]{1,0:T(8,128)(2,1)S(1)}, u32[]{:S(2)}, u32[]{:S(2)}) collective-permute-start(bf16[128,2304]{1,0:T(8,128)(2,1)S(1)} %collective-permute-done.1.refs_6_), channel_id=1, source_target_pairs={{0,1},{1,0},{2,3},{3,2},{4,5},{5,4},{6,7},{7,6},{8,9},{9,8},{10,11... | collective-permute-start | bytes 1769480 | tf_op jit(solution)/shard_map/ppermute | solution.py:358
  15.3 15.3 %collective-permute-start.5 = (bf16[8,32,512]{2,1,0:T(8,128)(2,1)S(1)}, bf16[8,32,512]{2,1,0:T(8,128)(2,1)S(1)}, u32[]{:S(2)}, u32[]{:S(2)}) collective-permute-start(bf16[8,32,512]{2,1,0:T(8,128)(2,1)S(1)} %get-tuple-element.35), channel_id=1, source_target_pairs={{0,64},{64,128},{128,192},{192,0},{1,65},{65,129},{129,193},{193,1... | collective-permute-start | bytes 786440 | tf_op jit(solution)/shard_map/ppermute | solution.py:363
  19.8 10.8 %collective-permute-start.6 = (bf16[8,32,512]{2,1,0:T(8,128)(2,1)S(1)}, bf16[8,32,512]{2,1,0:T(8,128)(2,1)S(1)}, u32[]{:S(2)}, u32[]{:S(2)}) collective-permute-start(bf16[8,32,512]{2,1,0:T(8,128)(2,1)S(1)} %get-tuple-element.36), channel_id=1, source_target_pairs={{0,192},{64,0},{128,64},{192,128},{1,193},{65,1},{129,65},{193,129... | collective-permute-start | bytes 786440 | tf_op jit(solution)/shard_map/ppermute | solution.py:363
  21.6 12.9 %collective-permute-start.7 = (bf16[8,32,512]{2,1,0:T(8,128)(2,1)S(1)}, bf16[8,32,512]{2,1,0:T(8,128)(2,1)S(1)}, u32[]{:S(2)}, u32[]{:S(2)}) collective-permute-start(bf16[8,32,512]{2,1,0:T(8,128)(2,1)S(1)} %get-tuple-element.37), channel_id=1, source_target_pairs={{0,64},{64,128},{128,192},{192,0},{1,65},{65,129},{129,193},{193,1... | collective-permute-start | bytes 786440 | tf_op jit(solution)/shard_map/ppermute | solution.py:363
  21.9 12.6 %collective-permute-start.8 = (bf16[8,32,512]{2,1,0:T(8,128)(2,1)S(1)}, bf16[8,32,512]{2,1,0:T(8,128)(2,1)S(1)}, u32[]{:S(2)}, u32[]{:S(2)}) collective-permute-start(bf16[8,32,512]{2,1,0:T(8,128)(2,1)S(1)} %get-tuple-element.38), channel_id=1, source_target_pairs={{0,192},{64,0},{128,64},{192,128},{1,193},{65,1},{129,65},{193,129... | collective-permute-start | bytes 786440 | tf_op jit(solution)/shard_map/ppermute | solution.py:363
  39.4 10.5 %copy-start.5 = (f32[1152]{0:T(1024)S(1)}, f32[1152]{0:T(1024)}, u32[]{:S(2)}) copy-start(f32[1152]{0:T(1024)} %param.14) | copy-start | bytes 13828
  39.4 40.0 %all-to-all-start = ((bf16[16,32,1152]{2,1,0:T(8,128)(2,1)}), bf16[16,32,1152]{2,1,0:T(8,128)(2,1)S(1)}, u32[]{:S(2)}, u32[]{:S(2)}) async-start(bf16[16,32,1152]{2,1,0:T(8,128)(2,1)} %bitcast.37), calls=%async_computation | async-start | bytes 2359296 | tf_op jit(solution)/shard_map/all_to_all | solution.py:367

commit v5 on v4

--- a/solution.py
+++ b/solution.py
@@ -72,11 +72,11 @@
     moves = []
     if last_step:
         at = 0
-        for index, ref in enumerate((*finished, state_ref)):
+        for ref in finished:
             columns = slice(at, at + ref.shape[1])
-            moves.append(pltpu.make_async_copy(ref, out_ref.at[:, columns], sems.at[index]))
+            moves.append(pltpu.make_async_copy(ref, out_ref.at[:, columns], sems.at[len(moves)]))
             at += ref.shape[1]
-        for move in moves[:-1]:
+        for move in moves:
             move.start()
 
     band = lax.axis_index("band")
@@ -150,18 +150,27 @@
             else:
                 mixed_ref[:, at - begin : at - begin + LANES] = part
                 done = at + LANES
+            if last_step and high >= at + LANES:
+                tile = slice(at - begin, at - begin + LANES)
+                state_ref[:, tile] = (
+                    hidden_ref[:, at : at + LANES].astype(jnp.float32) + mixed_ref[:, tile]
+                ).astype(jnp.bfloat16)
+                moves.append(
+                    pltpu.make_async_copy(
+                        state_ref.at[:, tile], out_ref.at[:, at : at + LANES],
+                        sems.at[len(moves)],
+                    )
+                )
+                moves[-1].start()
         scores = following
-    size = finish - begin if last_step else out_ref.shape[1]
-    state = (
-        hidden_ref[:, begin : begin + size].astype(jnp.float32) + mixed_ref[:, :size]
-    ).astype(jnp.bfloat16)
     if last_step:
-        state_ref[...] = state
-        moves[-1].start()
         for move in moves:
             move.wait()
     else:
-        out_ref[...] = state
+        size = out_ref.shape[1]
+        out_ref[...] = (
+            hidden_ref[:, begin : begin + size].astype(jnp.float32) + mixed_ref[:, :size]
+        ).astype(jnp.bfloat16)
     if not last_step:
         rest[1][...] = mixed_ref[:, size : size + LANES]
 
@@ -210,7 +219,7 @@
             pltpu.VMEM((keys, read - begin), jnp.bfloat16),
             pltpu.VMEM((keys, read - begin), jnp.bfloat16),
             pltpu.VMEM((tokens, width - begin if last_step else LANES), jnp.bfloat16),
-            pltpu.SemaphoreType.DMA((len(HEAD_STEPS) - 1,)),
+            pltpu.SemaphoreType.DMA((len(finished) + (width - begin) // LANES,)),
         ],
         compiler_params=pltpu.CompilerParams(vmem_limit_bytes=VMEM_LIMIT),
         name="cond_attention",

time: 128 us -> 128 us (level)
  no operation moved by 1% of the time
where the time goes in v5:
time: 128 us; the launch traced here: 126 us
  waiting for transfers between devices  41.1 us (32%)
  blocking collectives  34.6 us (27%)
  Pallas kernels  29.6 us (23%)
  starting transfers between devices  19.5 us (15%)
    all_to_all x1, blocking collectives, regroup(): lax.all_to_all(array, 'frame', split_axis=0, concat_axis=0, tiled=True)  34.6 us
    all_to_all x1, waiting for transfers between devices, regroup(): lax.all_to_all(array, 'frame', split_axis=0, concat_axis=0, tiled=True)  29.5 us
    pallas_call x3, Pallas kernels, cond_attention(): pl.pallas_call(functools.partial(cond_kernel, half, width, heads, cuts, l...  15.7 us
    pallas_call x1, Pallas kernels, temporal_attention(): pl.pallas_call(temporal_kernel, grid=(3,), in_specs=[whole, pl.BlockSpec(...  11 us
    all_to_all x1, starting transfers between devices, regroup(): lax.all_to_all(array, 'frame', split_axis=0, concat_axis=0, tiled=True)  10.5 us
    ppermute x3, waiting for transfers between devices, exchange(): return lax.ppermute(array, axis, [(i, i ^ flip) for i in range(length)])  8.64 us
    ppermute x6, starting transfers between devices, passed_along(): lax.ppermute(array, axis, [(i, (i + by) % length) for i in range(length)])  7.51 us
    ppermute x6, waiting for transfers between devices, passed_along(): lax.ppermute(array, axis, [(i, (i + by) % length) for i in range(length)])  3 us
  transfers between devices with their start and end apart: 10, of which 3 were waited for; matrix products, arithmetic and copies ran while one was open for 0% of the time, Pallas kernels for 11%

profile of v5, /device:TPU:8, one launch (start us, length us, event | category | flops | bytes accessed | tf_op | source)
XLA Modules:
  0.0 126.0 jit_solution(4947399697083544813)
XLA Ops:
  0.0 1.5 %collective-permute-start.1 = (bf16[128,2304]{1,0:T(8,128)(2,1)}, bf16[128,2304]{1,0:T(8,128)(2,1)S(1)}, u32[]{:S(2)}, u32[]{:S(2)}) collective-permute-start(bf16[128,2304]{1,0:T(8,128)(2,1)} %bitcast.24), channel_id=1, source_target_pairs={{0,2},{1,3},{2,0},{3,1},{4,6},{5,7},{6,4},{7,5},{8,10},{9,11},{10,... | collective-permute-start | bytes 1769480 | tf_op jit(solution)/shard_map/ppermute | solution.py:367
  1.5 1.4 %split_halves.3 = (bf16[8,32,1280]{2,1,0:T(8,128)(2,1)S(1)}, bf16[8,32,1280]{2,1,0:T(8,128)(2,1)S(1)}) custom-call(bf16[8,64,2304]{2,1,0:T(8,128)(2,1)} %bitcast.35), custom_call_target="tpu_custom_call" | custom-call | tf_op jit(solution)/shard_map/split_halves/pallas_call | solution.py:353
  2.9 1.7 %collective-permute-start.3 = (bf16[8,32,1280]{2,1,0:T(8,128)(2,1)S(1)}, bf16[8,32,1280]{2,1,0:T(8,128)(2,1)S(1)}, u32[]{:S(2)}, u32[]{:S(2)}) collective-permute-start(bf16[8,32,1280]{2,1,0:T(8,128)(2,1)S(1)} %get-tuple-element.31), channel_id=1, source_target_pairs={{0,64},{64,128},{128,192},{192,0},{1,65},{65,129},{129,193},{193,1... | collective-permute-start | bytes 1966088 | tf_op jit(solution)/shard_map/ppermute | solution.py:372
  4.5 0.5 collective-permute-start.4
  5.1 0.0 collective-permute-start
  5.1 1.6 %split_halves.2 = (bf16[8,32,512]{2,1,0:T(8,128)(2,1)S(1)}, bf16[8,32,512]{2,1,0:T(8,128)(2,1)S(1)}, bf16[8,32,512]{2,1,0:T(8,128)(2,1)S(1)}, bf16[8,32,512]{2,1,0:T(8,128)(2,1)S(1)}) custom-call(bf16[8,64,2304]{2,1,0:T(8,128)(2,1)} %bitcast.36), custom_call_target="tpu_custom_call" | custom-call | tf_op jit(solution)/shard_map/split_halves/pallas_call | solution.py:353
  6.6 8.6 %collective-permute-done.1.refs_6_ = bf16[128,2304]{1,0:T(8,128)(2,1)S(1)} collective-permute-done((bf16[128,2304]{1,0:T(8,128)(2,1)}, bf16[128,2304]{1,0:T(8,128)(2,1)S(1)}, u32[]{:S(2)}, u32[]{:S(2)}) %collective-permute-start.1) | collective-permute-done | bytes 589856 | tf_op jit(solution)/shard_map/ppermute | solution.py:367
  15.3 0.0 collective-permute-start.2
  15.3 1.6 %collective-permute-start.5 = (bf16[8,32,512]{2,1,0:T(8,128)(2,1)S(1)}, bf16[8,32,512]{2,1,0:T(8,128)(2,1)S(1)}, u32[]{:S(2)}, u32[]{:S(2)}) collective-permute-start(bf16[8,32,512]{2,1,0:T(8,128)(2,1)S(1)} %get-tuple-element.35), channel_id=1, source_target_pairs={{0,64},{64,128},{128,192},{192,0},{1,65},{65,129},{129,193},{193,1... | collective-permute-start | bytes 786440 | tf_op jit(solution)/shard_map/ppermute | solution.py:372
  16.9 3.0 %collective-permute-done.3 = bf16[8,32,1280]{2,1,0:T(8,128)(2,1)S(1)} collective-permute-done((bf16[8,32,1280]{2,1,0:T(8,128)(2,1)S(1)}, bf16[8,32,1280]{2,1,0:T(8,128)(2,1)S(1)}, u32[]{:S(2)}, u32[]{:S(2)}) %collective-permute-start.3) | collective-permute-done | bytes 655392 | tf_op jit(solution)/shard_map/ppermute | solution.py:372
  19.8 1.7 %collective-permute-start.6 = (bf16[8,32,512]{2,1,0:T(8,128)(2,1)S(1)}, bf16[8,32,512]{2,1,0:T(8,128)(2,1)S(1)}, u32[]{:S(2)}, u32[]{:S(2)}) collective-permute-start(bf16[8,32,512]{2,1,0:T(8,128)(2,1)S(1)} %get-tuple-element.36), channel_id=1, source_target_pairs={{0,192},{64,0},{128,64},{192,128},{1,193},{65,1},{129,65},{193,129... | collective-permute-start | bytes 786440 | tf_op jit(solution)/shard_map/ppermute | solution.py:372
  21.6 0.3 collective-permute-start.7
  21.9 0.0 collective-permute-done.refs_5_
  21.9 1.7 %collective-permute-start.8 = (bf16[8,32,512]{2,1,0:T(8,128)(2,1)S(1)}, bf16[8,32,512]{2,1,0:T(8,128)(2,1)S(1)}, u32[]{:S(2)}, u32[]{:S(2)}) collective-permute-start(bf16[8,32,512]{2,1,0:T(8,128)(2,1)S(1)} %get-tuple-element.38), channel_id=1, source_target_pairs={{0,192},{64,0},{128,64},{192,128},{1,193},{65,1},{129,65},{193,129... | collective-permute-start | bytes 786440 | tf_op jit(solution)/shard_map/ppermute | solution.py:372
  23.6 0.0 collective-permute-done.2.refs_7_
  23.6 7.0 %cond_attention.3 = (bf16[512,512]{1,0:T(8,128)(2,1)S(1)}, f32[512,128]{1,0:T(8,128)S(1)}) custom-call(s32[1,4]{1,0:T(1,128)S(1)} %copy-done.3, s32[1,2]{1,0:T(1,128)S(1)} %copy-done.4, bf16[512,1152]{1,0:T(8,128)(2,1)S(1)} %bitcast.12, bf16[512,1152]{1,0:T(8,128)(2,1)S(1)} %bitcast.15, bf16[128,2304]{1,0:T(8,128)(2,1)S(1)} %bitcast.26, ...), custom_call_target="tpu_custom_call" | custom-call | tf_op jit(solution)/shard_map/cond_attention/pallas_call | solution.py:211
  30.7 3.9 %cond_attention.4 = (bf16[512,256]{1,0:T(8,128)(2,1)S(1)}, f32[512,128]{1,0:T(8,128)S(1)}) custom-call(s32[1,4]{1,0:T(1,128)S(1)} %copy-done.3, s32[1,2]{1,0:T(1,128)S(1)} %copy-done.4, bf16[512,1152]{1,0:T(8,128)(2,1)S(1)} %bitcast.13, bf16[512,1152]{1,0:T(8,128)(2,1)S(1)} %bitcast.16, bf16[128,2304]{1,0:T(8,128)(2,1)S(1)} %bitcast.27, ...), custom_call_target="tpu_custom_call" | custom-call | tf_op jit(solution)/shard_map/cond_attention/pallas_call | solution.py:211
  34.6 4.8 %cond_attention.5 = bf16[512,1152]{1,0:T(8,128)(2,1)} custom-call(s32[1,4]{1,0:T(1,128)S(1)} %copy-done.3, s32[1,2]{1,0:T(1,128)S(1)} %copy-done.4, bf16[512,1152]{1,0:T(8,128)(2,1)S(1)} %bitcast.14, bf16[512,1152]{1,0:T(8,128)(2,1)S(1)} %bitcast.17, bf16[128,2304]{1,0:T(8,128)(2,1)S(1)} %bitcast.28, bf16[128,2304]{1,0:T(8,128)(2,1)S(1)} %collective-permute-done.refs_5_, ...), custom_call_target="tpu_custom_call" | custom-call | tf_op jit(solution)/shard_map/cond_attention/pallas_call | solution.py:211
  39.4 0.0 copy-start.5
  39.4 10.5 %all-to-all-start = ((bf16[16,32,1152]{2,1,0:T(8,128)(2,1)}), bf16[16,32,1152]{2,1,0:T(8,128)(2,1)S(1)}, u32[]{:S(2)}, u32[]{:S(2)}) async-start(bf16[16,32,1152]{2,1,0:T(8,128)(2,1)} %bitcast.37), calls=%async_computation | async-start | bytes 2359296 | tf_op jit(solution)/shard_map/all_to_all | solution.py:376
  49.9 29.5 %all-to-all-done.x_ref = bf16[16,32,1152]{2,1,0:T(8,128)(2,1)S(1)} async-done(((bf16[16,32,1152]{2,1,0:T(8,128)(2,1)}), bf16[16,32,1152]{2,1,0:T(8,128)(2,1)S(1)}, u32[]{:S(2)}, u32[]{:S(2)}) %all-to-all-start) | async-done | bytes 1179680 | tf_op jit(solution)/shard_map/all_to_all | solution.py:376
  79.4 11.0 %temporal_attention.1 = bf16[16,32,1152]{2,1,0:T(8,128)(2,1)S(1)} custom-call(bf16[16,32,1152]{2,1,0:T(8,128)(2,1)S(1)} %all-to-all-done.x_ref, f32[1,1152]{1,0:T(1,128)S(1)} %reshape.34.gain_ref, bf16[1152,3456]{1,0:T(8,128)(2,1)} %w_ref.1), custom_call_target="tpu_custom_call" | custom-call | tf_op jit(solution)/shard_map/temporal_attention/pallas_call | solution.py:299
  90.4 34.6 %all_to_all.10 = bf16[16,32,1152]{2,1,0:T(8,128)(2,1)S(1)} all-to-all(bf16[16,32,1152]{2,1,0:T(8,128)(2,1)S(1)} %temporal_attention.1), channel_id=1, replica_groups=mesh['view'=4,'frame'=16,'band'=4] {'frame'}, dimensions={0} | all-to-all | bytes 2359296 | tf_op jit(solution)/shard_map/all_to_all | solution.py:376
  125.0 1.0 copy.10
  (17 shorter events, 0.0 us)
Async XLA Ops:
  0.0 15.3 %collective-permute-start.1 = (bf16[128,2304]{1,0:T(8,128)(2,1)}, bf16[128,2304]{1,0:T(8,128)(2,1)S(1)}, u32[]{:S(2)}, u32[]{:S(2)}) collective-permute-start(bf16[128,2304]{1,0:T(8,128)(2,1)} %bitcast.24), channel_id=1, source_target_pairs={{0,2},{1,3},{2,0},{3,1},{4,6},{5,7},{6,4},{7,5},{8,10},{9,11},{10,... | collective-permute-start | bytes 1769480 | tf_op jit(solution)/shard_map/ppermute | solution.py:367
  1.5 3.6 %copy-start.2 = (bf16[1,128,2304]{2,1,0:T(8,128)(2,1)S(1)}, bf16[1,128,2304]{2,1,0:T(8,128)(2,1)}, u32[]{:S(2)}) copy-start(bf16[1,128,2304]{2,1,0:T(8,128)(2,1)} %param.11) | copy-start | bytes 1769476
  2.9 17.0 %collective-permute-start.3 = (bf16[8,32,1280]{2,1,0:T(8,128)(2,1)S(1)}, bf16[8,32,1280]{2,1,0:T(8,128)(2,1)S(1)}, u32[]{:S(2)}, u32[]{:S(2)}) collective-permute-start(bf16[8,32,1280]{2,1,0:T(8,128)(2,1)S(1)} %get-tuple-element.31), channel_id=1, source_target_pairs={{0,64},{64,128},{128,192},{192,0},{1,65},{65,129},{129,193},{193,1... | collective-permute-start | bytes 1966088 | tf_op jit(solution)/shard_map/ppermute | solution.py:372
  4.5 19.1 %copy-start = (bf16[1,1,8,64,1152]{4,3,2,1,0:T(8,128)(2,1)S(1)}, bf16[1,1,8,64,1152]{4,3,2,1,0:T(8,128)(2,1)}, u32[]{:S(2)}) copy-start(bf16[1,1,8,64,1152]{4,3,2,1,0:T(8,128)(2,1)} %param.9) | copy-start | bytes 3538948
  4.5 19.1 %copy-start.1 = (bf16[1,1,8,64,1152]{4,3,2,1,0:T(8,128)(2,1)S(1)}, bf16[1,1,8,64,1152]{4,3,2,1,0:T(8,128)(2,1)}, u32[]{:S(2)}) copy-start(bf16[1,1,8,64,1152]{4,3,2,1,0:T(8,128)(2,1)} %param.8) | copy-start | bytes 3538948
  4.5 19.1 %copy-start.3 = (s32[1,4]{1,0:T(1,128)S(1)}, s32[1,4]{1,0:T(1,128)}, u32[]{:S(2)}) copy-start(s32[1,4]{1,0:T(1,128)} %refs_0_.5) | copy-start | bytes 52
  4.5 19.1 %copy-start.4 = (s32[1,2]{1,0:T(1,128)S(1)}, s32[1,2]{1,0:T(1,128)}, u32[]{:S(2)}) copy-start(s32[1,2]{1,0:T(1,128)} %refs_1_.5) | copy-start | bytes 28
  4.5 17.0 %collective-permute-start.4 = (bf16[8,32,1280]{2,1,0:T(8,128)(2,1)S(1)}, bf16[8,32,1280]{2,1,0:T(8,128)(2,1)S(1)}, u32[]{:S(2)}, u32[]{:S(2)}) collective-permute-start(bf16[8,32,1280]{2,1,0:T(8,128)(2,1)S(1)} %get-tuple-element.32), channel_id=1, source_target_pairs={{0,192},{64,0},{128,64},{192,128},{1,193},{65,1},{129,65},{193,129... | collective-permute-start | bytes 1966088 | tf_op jit(solution)/shard_map/ppermute | solution.py:372
  5.1 16.8 %collective-permute-start = (bf16[128,2304]{1,0:T(8,128)(2,1)S(1)}, bf16[128,2304]{1,0:T(8,128)(2,1)S(1)}, u32[]{:S(2)}, u32[]{:S(2)}) collective-permute-start(bf16[128,2304]{1,0:T(8,128)(2,1)S(1)} %bitcast.25), channel_id=1, source_target_pairs={{0,1},{1,0},{2,3},{3,2},{4,5},{5,4},{6,7},{7,6},{8,9},{9,8},{10,11... | collective-permute-start | bytes 1769480 | tf_op jit(solution)/shard_map/ppermute | solution.py:367
  15.3 8.3 %collective-permute-start.2 = (bf16[128,2304]{1,0:T(8,128)(2,1)S(1)}, bf16[128,2304]{1,0:T(8,128)(2,1)S(1)}, u32[]{:S(2)}, u32[]{:S(2)}) collective-permute-start(bf16[128,2304]{1,0:T(8,128)(2,1)S(1)} %collective-permute-done.1.refs_6_), channel_id=1, source_target_pairs={{0,1},{1,0},{2,3},{3,2},{4,5},{5,4},{6,7},{7,6},{8,9},{9,8},{10,11... | collective-permute-start | bytes 1769480 | tf_op jit(solution)/shard_map/ppermute | solution.py:367
  15.3 15.4 %collective-permute-start.5 = (bf16[8,32,512]{2,1,0:T(8,128)(2,1)S(1)}, bf16[8,32,512]{2,1,0:T(8,128)(2,1)S(1)}, u32[]{:S(2)}, u32[]{:S(2)}) collective-permute-start(bf16[8,32,512]{2,1,0:T(8,128)(2,1)S(1)} %get-tuple-element.35), channel_id=1, source_target_pairs={{0,64},{64,128},{128,192},{192,0},{1,65},{65,129},{129,193},{193,1... | collective-permute-start | bytes 786440 | tf_op jit(solution)/shard_map/ppermute | solution.py:372
  19.8 10.8 %collective-permute-start.6 = (bf16[8,32,512]{2,1,0:T(8,128)(2,1)S(1)}, bf16[8,32,512]{2,1,0:T(8,128)(2,1)S(1)}, u32[]{:S(2)}, u32[]{:S(2)}) collective-permute-start(bf16[8,32,512]{2,1,0:T(8,128)(2,1)S(1)} %get-tuple-element.36), channel_id=1, source_target_pairs={{0,192},{64,0},{128,64},{192,128},{1,193},{65,1},{129,65},{193,129... | collective-permute-start | bytes 786440 | tf_op jit(solution)/shard_map/ppermute | solution.py:372
  21.6 13.0 %collective-permute-start.7 = (bf16[8,32,512]{2,1,0:T(8,128)(2,1)S(1)}, bf16[8,32,512]{2,1,0:T(8,128)(2,1)S(1)}, u32[]{:S(2)}, u32[]{:S(2)}) collective-permute-start(bf16[8,32,512]{2,1,0:T(8,128)(2,1)S(1)} %get-tuple-element.37), channel_id=1, source_target_pairs={{0,64},{64,128},{128,192},{192,0},{1,65},{65,129},{129,193},{193,1... | collective-permute-start | bytes 786440 | tf_op jit(solution)/shard_map/ppermute | solution.py:372
  21.9 12.7 %collective-permute-start.8 = (bf16[8,32,512]{2,1,0:T(8,128)(2,1)S(1)}, bf16[8,32,512]{2,1,0:T(8,128)(2,1)S(1)}, u32[]{:S(2)}, u32[]{:S(2)}) collective-permute-start(bf16[8,32,512]{2,1,0:T(8,128)(2,1)S(1)} %get-tuple-element.38), channel_id=1, source_target_pairs={{0,192},{64,0},{128,64},{192,128},{1,193},{65,1},{129,65},{193,129... | collective-permute-start | bytes 786440 | tf_op jit(solution)/shard_map/ppermute | solution.py:372
  39.4 10.5 %copy-start.5 = (f32[1152]{0:T(1024)S(1)}, f32[1152]{0:T(1024)}, u32[]{:S(2)}) copy-start(f32[1152]{0:T(1024)} %param.14) | copy-start | bytes 13828
  39.4 40.0 %all-to-all-start = ((bf16[16,32,1152]{2,1,0:T(8,128)(2,1)}), bf16[16,32,1152]{2,1,0:T(8,128)(2,1)S(1)}, u32[]{:S(2)}, u32[]{:S(2)}) async-start(bf16[16,32,1152]{2,1,0:T(8,128)(2,1)} %bitcast.37), calls=%async_computation | async-start | bytes 2359296 | tf_op jit(solution)/shard_map/all_to_all | solution.py:376

commit v6 on v5

--- a/solution.py
+++ b/solution.py
@@ -394,6 +394,7 @@
 
     layout = layout_kv[0]
     (first_source,) = split_halves(own, cuts[:2])
+    first_source, layout = lax.optimization_barrier((first_source, layout))
     first = sent(first_source)
     across = exchange(layout, "band", 2)
     beside = exchange(layout, "band", 1)

time: 128 us -> 128 us (level)
    ppermute x6, waiting for transfers between devices: 3 us -> 1.05 us  [passed_along(): lax.ppermute(array, axis, [(i, (i + by) % length) for i in range(length)])]
    ppermute x3, waiting for transfers between devices: 8.64 us -> 10.2 us  [exchange(): return lax.ppermute(array, axis, [(i, i ^ flip) for i in range(length)])]
  transfers between devices with their start and end apart: 10 -> 10, of which waited for: 3 -> 3; matrix products, arithmetic and copies ran while one was open for 0% -> 0% of each run, Pallas kernels for 11% -> 10%
where the time goes in v6:
time: 128 us; the launch traced here: 126 us
  waiting for transfers between devices  41.1 us (32%)
  blocking collectives  34.6 us (27%)
  Pallas kernels  29.4 us (23%)
  starting transfers between devices  19.7 us (15%)
    all_to_all x1, blocking collectives, regroup(): lax.all_to_all(array, 'frame', split_axis=0, concat_axis=0, tiled=True)  34.6 us
    all_to_all x1, waiting for transfers between devices, regroup(): lax.all_to_all(array, 'frame', split_axis=0, concat_axis=0, tiled=True)  29.9 us
    pallas_call x3, Pallas kernels, cond_attention(): pl.pallas_call(functools.partial(cond_kernel, half, width, heads, cuts, l...  15.7 us
    pallas_call x1, Pallas kernels, temporal_attention(): pl.pallas_call(temporal_kernel, grid=(3,), in_specs=[whole, pl.BlockSpec(...  11 us
    all_to_all x1, starting transfers between devices, regroup(): lax.all_to_all(array, 'frame', split_axis=0, concat_axis=0, tiled=True)  10.7 us
    ppermute x3, waiting for transfers between devices, exchange(): return lax.ppermute(array, axis, [(i, i ^ flip) for i in range(length)])  10.2 us
    ppermute x6, starting transfers between devices, passed_along(): lax.ppermute(array, axis, [(i, (i + by) % length) for i in range(length)])  7.37 us
    pallas_call x2, Pallas kernels, split_halves(): pl.pallas_call(functools.partial(split_kernel, columns // 2, cuts), in_sp...  2.74 us
  transfers between devices with their start and end apart: 10, of which 3 were waited for; matrix products, arithmetic and copies ran while one was open for 0% of the time, Pallas kernels for 10%

profile of v6, /device:TPU:8, one launch (start us, length us, event | category | flops | bytes accessed | tf_op | source)
XLA Modules:
  0.0 126.2 jit_solution(16056871710538890721)
XLA Ops:
  0.0 1.4 %split_halves.2 = (bf16[8,32,1280]{2,1,0:T(8,128)(2,1)S(1)}, bf16[8,32,1280]{2,1,0:T(8,128)(2,1)S(1)}) custom-call(bf16[8,64,2304]{2,1,0:T(8,128)(2,1)} %bitcast.35), custom_call_target="tpu_custom_call" | custom-call | tf_op jit(solution)/shard_map/split_halves/pallas_call | solution.py:353
  1.4 0.1 copy-done.2
  1.5 1.6 %collective-permute-start.1 = (bf16[128,2304]{1,0:T(8,128)(2,1)S(1)}, bf16[128,2304]{1,0:T(8,128)(2,1)S(1)}, u32[]{:S(2)}, u32[]{:S(2)}) collective-permute-start(bf16[128,2304]{1,0:T(8,128)(2,1)S(1)} %bitcast.24), channel_id=1, source_target_pairs={{0,2},{1,3},{2,0},{3,1},{4,6},{5,7},{6,4},{7,5},{8,10},{9,11},{10,... | collective-permute-start | bytes 1769480 | tf_op jit(solution)/shard_map/ppermute | solution.py:367
  3.1 1.6 %collective-permute-start.3 = (bf16[8,32,1280]{2,1,0:T(8,128)(2,1)S(1)}, bf16[8,32,1280]{2,1,0:T(8,128)(2,1)S(1)}, u32[]{:S(2)}, u32[]{:S(2)}) collective-permute-start(bf16[8,32,1280]{2,1,0:T(8,128)(2,1)S(1)} %get-tuple-element.37), channel_id=1, source_target_pairs={{0,64},{64,128},{128,192},{192,0},{1,65},{65,129},{129,193},{193,1... | collective-permute-start | bytes 1966088 | tf_op jit(solution)/shard_map/ppermute | solution.py:372
  4.6 0.4 collective-permute-start.4
  5.1 0.0 collective-permute-start
  5.1 1.4 %split_halves.3 = (bf16[8,32,512]{2,1,0:T(8,128)(2,1)S(1)}, bf16[8,32,512]{2,1,0:T(8,128)(2,1)S(1)}, bf16[8,32,512]{2,1,0:T(8,128)(2,1)S(1)}, bf16[8,32,512]{2,1,0:T(8,128)(2,1)S(1)}) custom-call(bf16[8,64,2304]{2,1,0:T(8,128)(2,1)} %bitcast.36), custom_call_target="tpu_custom_call" | custom-call | tf_op jit(solution)/shard_map/split_halves/pallas_call | solution.py:353
  6.5 10.2 %collective-permute-done.1.refs_6_ = bf16[128,2304]{1,0:T(8,128)(2,1)S(1)} collective-permute-done((bf16[128,2304]{1,0:T(8,128)(2,1)S(1)}, bf16[128,2304]{1,0:T(8,128)(2,1)S(1)}, u32[]{:S(2)}, u32[]{:S(2)}) %collective-permute-start.1) | collective-permute-done | bytes 589856 | tf_op jit(solution)/shard_map/ppermute | solution.py:367
  16.6 0.0 collective-permute-start.2
  16.6 1.6 %collective-permute-start.5 = (bf16[8,32,512]{2,1,0:T(8,128)(2,1)S(1)}, bf16[8,32,512]{2,1,0:T(8,128)(2,1)S(1)}, u32[]{:S(2)}, u32[]{:S(2)}) collective-permute-start(bf16[8,32,512]{2,1,0:T(8,128)(2,1)S(1)} %get-tuple-element.41), channel_id=1, source_target_pairs={{0,64},{64,128},{128,192},{192,0},{1,65},{65,129},{129,193},{193,1... | collective-permute-start | bytes 786440 | tf_op jit(solution)/shard_map/ppermute | solution.py:372
  18.2 1.0 collective-permute-done.3
  19.2 1.7 %collective-permute-start.6 = (bf16[8,32,512]{2,1,0:T(8,128)(2,1)S(1)}, bf16[8,32,512]{2,1,0:T(8,128)(2,1)S(1)}, u32[]{:S(2)}, u32[]{:S(2)}) collective-permute-start(bf16[8,32,512]{2,1,0:T(8,128)(2,1)S(1)} %get-tuple-element.42), channel_id=1, source_target_pairs={{0,192},{64,0},{128,64},{192,128},{1,193},{65,1},{129,65},{193,129... | collective-permute-start | bytes 786440 | tf_op jit(solution)/shard_map/ppermute | solution.py:372
  21.0 0.0 collective-permute-done.4
  21.0 0.8 collective-permute-start.7
  21.8 1.2 collective-permute-start.8
  23.1 7.0 %cond_attention.3 = (bf16[512,512]{1,0:T(8,128)(2,1)S(1)}, f32[512,128]{1,0:T(8,128)S(1)}) custom-call(s32[1,4]{1,0:T(1,128)S(1)} %copy-done.3, s32[1,2]{1,0:T(1,128)S(1)} %copy-done.4, bf16[512,1152]{1,0:T(8,128)(2,1)S(1)} %bitcast.12, bf16[512,1152]{1,0:T(8,128)(2,1)S(1)} %bitcast.15, bf16[128,2304]{1,0:T(8,128)(2,1)S(1)} %bitcast.26, ...), custom_call_target="tpu_custom_call" | custom-call | tf_op jit(solution)/shard_map/cond_attention/pallas_call | solution.py:211
  30.1 3.9 %cond_attention.4 = (bf16[512,256]{1,0:T(8,128)(2,1)S(1)}, f32[512,128]{1,0:T(8,128)S(1)}) custom-call(s32[1,4]{1,0:T(1,128)S(1)} %copy-done.3, s32[1,2]{1,0:T(1,128)S(1)} %copy-done.4, bf16[512,1152]{1,0:T(8,128)(2,1)S(1)} %bitcast.13, bf16[512,1152]{1,0:T(8,128)(2,1)S(1)} %bitcast.16, bf16[128,2304]{1,0:T(8,128)(2,1)S(1)} %bitcast.27, ...), custom_call_target="tpu_custom_call" | custom-call | tf_op jit(solution)/shard_map/cond_attention/pallas_call | solution.py:211
  34.0 4.8 %cond_attention.5 = bf16[512,1152]{1,0:T(8,128)(2,1)} custom-call(s32[1,4]{1,0:T(1,128)S(1)} %copy-done.3, s32[1,2]{1,0:T(1,128)S(1)} %copy-done.4, bf16[512,1152]{1,0:T(8,128)(2,1)S(1)} %bitcast.14, bf16[512,1152]{1,0:T(8,128)(2,1)S(1)} %bitcast.17, bf16[128,2304]{1,0:T(8,128)(2,1)S(1)} %bitcast.28, bf16[128,2304]{1,0:T(8,128)(2,1)S(1)} %collective-permute-done.refs_5_, ...), custom_call_target="tpu_custom_call" | custom-call | tf_op jit(solution)/shard_map/cond_attention/pallas_call | solution.py:211
  38.9 0.0 copy-start.5
  38.9 10.7 %all-to-all-start = ((bf16[16,32,1152]{2,1,0:T(8,128)(2,1)}), bf16[16,32,1152]{2,1,0:T(8,128)(2,1)S(1)}, u32[]{:S(2)}, u32[]{:S(2)}) async-start(bf16[16,32,1152]{2,1,0:T(8,128)(2,1)} %bitcast.37), calls=%async_computation | async-start | bytes 2359296 | tf_op jit(solution)/shard_map/all_to_all | solution.py:376
  49.6 29.9 %all-to-all-done.x_ref = bf16[16,32,1152]{2,1,0:T(8,128)(2,1)S(1)} async-done(((bf16[16,32,1152]{2,1,0:T(8,128)(2,1)}), bf16[16,32,1152]{2,1,0:T(8,128)(2,1)S(1)}, u32[]{:S(2)}, u32[]{:S(2)}) %all-to-all-start) | async-done | bytes 1179680 | tf_op jit(solution)/shard_map/all_to_all | solution.py:376
  79.5 11.0 %temporal_attention.1 = bf16[16,32,1152]{2,1,0:T(8,128)(2,1)S(1)} custom-call(bf16[16,32,1152]{2,1,0:T(8,128)(2,1)S(1)} %all-to-all-done.x_ref, f32[1,1152]{1,0:T(1,128)S(1)} %reshape.34.gain_ref, bf16[1152,3456]{1,0:T(8,128)(2,1)} %w_ref.1), custom_call_target="tpu_custom_call" | custom-call | tf_op jit(solution)/shard_map/temporal_attention/pallas_call | solution.py:299
  90.5 34.6 %all_to_all.10 = bf16[16,32,1152]{2,1,0:T(8,128)(2,1)S(1)} all-to-all(bf16[16,32,1152]{2,1,0:T(8,128)(2,1)S(1)} %temporal_attention.1), channel_id=1, replica_groups=mesh['view'=4,'frame'=16,'band'=4] {'frame'}, dimensions={0} | all-to-all | bytes 2359296 | tf_op jit(solution)/shard_map/all_to_all | solution.py:376
  125.1 1.0 copy.10
  (17 shorter events, 0.0 us)
Async XLA Ops:
  0.0 1.5 %copy-start.2 = (bf16[1,128,2304]{2,1,0:T(8,128)(2,1)S(1)}, bf16[1,128,2304]{2,1,0:T(8,128)(2,1)}, u32[]{:S(2)}) copy-start(bf16[1,128,2304]{2,1,0:T(8,128)(2,1)} %param.11) | copy-start | bytes 1769476
  1.5 21.6 %copy-start = (bf16[1,1,8,64,1152]{4,3,2,1,0:T(8,128)(2,1)S(1)}, bf16[1,1,8,64,1152]{4,3,2,1,0:T(8,128)(2,1)}, u32[]{:S(2)}) copy-start(bf16[1,1,8,64,1152]{4,3,2,1,0:T(8,128)(2,1)} %param.9) | copy-start | bytes 3538948
  1.5 21.6 %copy-start.1 = (bf16[1,1,8,64,1152]{4,3,2,1,0:T(8,128)(2,1)S(1)}, bf16[1,1,8,64,1152]{4,3,2,1,0:T(8,128)(2,1)}, u32[]{:S(2)}) copy-start(bf16[1,1,8,64,1152]{4,3,2,1,0:T(8,128)(2,1)} %param.8) | copy-start | bytes 3538948
  1.5 21.6 %copy-start.3 = (s32[1,4]{1,0:T(1,128)S(1)}, s32[1,4]{1,0:T(1,128)}, u32[]{:S(2)}) copy-start(s32[1,4]{1,0:T(1,128)} %refs_0_.5) | copy-start | bytes 52
  1.5 21.6 %copy-start.4 = (s32[1,2]{1,0:T(1,128)S(1)}, s32[1,2]{1,0:T(1,128)}, u32[]{:S(2)}) copy-start(s32[1,2]{1,0:T(1,128)} %refs_1_.5) | copy-start | bytes 28
  1.5 15.2 %collective-permute-start.1 = (bf16[128,2304]{1,0:T(8,128)(2,1)S(1)}, bf16[128,2304]{1,0:T(8,128)(2,1)S(1)}, u32[]{:S(2)}, u32[]{:S(2)}) collective-permute-start(bf16[128,2304]{1,0:T(8,128)(2,1)S(1)} %bitcast.24), channel_id=1, source_target_pairs={{0,2},{1,3},{2,0},{3,1},{4,6},{5,7},{6,4},{7,5},{8,10},{9,11},{10,... | collective-permute-start | bytes 1769480 | tf_op jit(solution)/shard_map/ppermute | solution.py:367
  3.1 16.2 %collective-permute-start.3 = (bf16[8,32,1280]{2,1,0:T(8,128)(2,1)S(1)}, bf16[8,32,1280]{2,1,0:T(8,128)(2,1)S(1)}, u32[]{:S(2)}, u32[]{:S(2)}) collective-permute-start(bf16[8,32,1280]{2,1,0:T(8,128)(2,1)S(1)} %get-tuple-element.37), channel_id=1, source_target_pairs={{0,64},{64,128},{128,192},{192,0},{1,65},{65,129},{129,193},{193,1... | collective-permute-start | bytes 1966088 | tf_op jit(solution)/shard_map/ppermute | solution.py:372
  4.6 16.4 %collective-permute-start.4 = (bf16[8,32,1280]{2,1,0:T(8,128)(2,1)S(1)}, bf16[8,32,1280]{2,1,0:T(8,128)(2,1)S(1)}, u32[]{:S(2)}, u32[]{:S(2)}) collective-permute-start(bf16[8,32,1280]{2,1,0:T(8,128)(2,1)S(1)} %get-tuple-element.38), channel_id=1, source_target_pairs={{0,192},{64,0},{128,64},{192,128},{1,193},{65,1},{129,65},{193,129... | collective-permute-start | bytes 1966088 | tf_op jit(solution)/shard_map/ppermute | solution.py:372
  5.1 16.7 %collective-permute-start = (bf16[128,2304]{1,0:T(8,128)(2,1)S(1)}, bf16[128,2304]{1,0:T(8,128)(2,1)S(1)}, u32[]{:S(2)}, u32[]{:S(2)}) collective-permute-start(bf16[128,2304]{1,0:T(8,128)(2,1)S(1)} %bitcast.25), channel_id=1, source_target_pairs={{0,1},{1,0},{2,3},{3,2},{4,5},{5,4},{6,7},{7,6},{8,9},{9,8},{10,11... | collective-permute-start | bytes 1769480 | tf_op jit(solution)/shard_map/ppermute | solution.py:367
  16.6 6.4 %collective-permute-start.2 = (bf16[128,2304]{1,0:T(8,128)(2,1)S(1)}, bf16[128,2304]{1,0:T(8,128)(2,1)S(1)}, u32[]{:S(2)}, u32[]{:S(2)}) collective-permute-start(bf16[128,2304]{1,0:T(8,128)(2,1)S(1)} %collective-permute-done.1.refs_6_), channel_id=1, source_target_pairs={{0,1},{1,0},{2,3},{3,2},{4,5},{5,4},{6,7},{7,6},{8,9},{9,8},{10,11... | collective-permute-start | bytes 1769480 | tf_op jit(solution)/shard_map/ppermute | solution.py:367
  16.6 13.5 %collective-permute-start.5 = (bf16[8,32,512]{2,1,0:T(8,128)(2,1)S(1)}, bf16[8,32,512]{2,1,0:T(8,128)(2,1)S(1)}, u32[]{:S(2)}, u32[]{:S(2)}) collective-permute-start(bf16[8,32,512]{2,1,0:T(8,128)(2,1)S(1)} %get-tuple-element.41), channel_id=1, source_target_pairs={{0,64},{64,128},{128,192},{192,0},{1,65},{65,129},{129,193},{193,1... | collective-permute-start | bytes 786440 | tf_op jit(solution)/shard_map/ppermute | solution.py:372
  19.2 10.8 %collective-permute-start.6 = (bf16[8,32,512]{2,1,0:T(8,128)(2,1)S(1)}, bf16[8,32,512]{2,1,0:T(8,128)(2,1)S(1)}, u32[]{:S(2)}, u32[]{:S(2)}) collective-permute-start(bf16[8,32,512]{2,1,0:T(8,128)(2,1)S(1)} %get-tuple-element.42), channel_id=1, source_target_pairs={{0,192},{64,0},{128,64},{192,128},{1,193},{65,1},{129,65},{193,129... | collective-permute-start | bytes 786440 | tf_op jit(solution)/shard_map/ppermute | solution.py:372
  21.0 13.0 %collective-permute-start.7 = (bf16[8,32,512]{2,1,0:T(8,128)(2,1)S(1)}, bf16[8,32,512]{2,1,0:T(8,128)(2,1)S(1)}, u32[]{:S(2)}, u32[]{:S(2)}) collective-permute-start(bf16[8,32,512]{2,1,0:T(8,128)(2,1)S(1)} %get-tuple-element.43), channel_id=1, source_target_pairs={{0,64},{64,128},{128,192},{192,0},{1,65},{65,129},{129,193},{193,1... | collective-permute-start | bytes 786440 | tf_op jit(solution)/shard_map/ppermute | solution.py:372
  21.8 12.2 %collective-permute-start.8 = (bf16[8,32,512]{2,1,0:T(8,128)(2,1)S(1)}, bf16[8,32,512]{2,1,0:T(8,128)(2,1)S(1)}, u32[]{:S(2)}, u32[]{:S(2)}) collective-permute-start(bf16[8,32,512]{2,1,0:T(8,128)(2,1)S(1)} %get-tuple-element.44), channel_id=1, source_target_pairs={{0,192},{64,0},{128,64},{192,128},{1,193},{65,1},{129,65},{193,129... | collective-permute-start | bytes 786440 | tf_op jit(solution)/shard_map/ppermute | solution.py:372
  38.9 10.8 %copy-start.5 = (f32[1152]{0:T(1024)S(1)}, f32[1152]{0:T(1024)}, u32[]{:S(2)}) copy-start(f32[1152]{0:T(1024)} %param.14) | copy-start | bytes 13828
  38.9 40.7 %all-to-all-start = ((bf16[16,32,1152]{2,1,0:T(8,128)(2,1)}), bf16[16,32,1152]{2,1,0:T(8,128)(2,1)S(1)}, u32[]{:S(2)}, u32[]{:S(2)}) async-start(bf16[16,32,1152]{2,1,0:T(8,128)(2,1)} %bitcast.37), calls=%async_computation | async-start | bytes 2359296 | tf_op jit(solution)/shard_map/all_to_all | solution.py:376
